TPU v7x, 32 devices: a whole 2x2x4 slice. The times are simulated.
32 devices in a mesh: dp: 16 (over z, y, x), sub: 2 (over core).
Axes of the slice: x: 2, y: 2, z: 4, core: 2. Of those that a mesh axis runs over, the one named last changes fastest.
Arguments:
- tokens: bfloat16 [128, 2048, 768], P(('dp', 'sub')), may hold values from -6 to 6
- doc_lengths: int32 [128, 16], P(('dp', 'sub')), may hold values from 1 to 2033, as said below
- selected: int32 [128, 256], P(('dp', 'sub')), may hold values from 0 to 2047, as said below
- w_router: bfloat16 [768], replicated, may hold values from -0.21875 to 0.21875
- gain_attn: bfloat16 [768], replicated, may hold values from 0.099609375 to 1.8984375
- w_qkv: bfloat16 [768, 2304], replicated, may hold values from -0.21875 to 0.21875
- w_out: bfloat16 [768, 768], replicated, may hold values from -0.875 to 0.875
- gain_mlp: bfloat16 [768], replicated, may hold values from 0.099609375 to 1.8984375
- w_up: bfloat16 [768, 3072], replicated, may hold values from -0.21875 to 0.21875
- b_up: bfloat16 [3072], replicated, may hold values from -3 to 3
- w_down: bfloat16 [3072, 768], replicated, may hold values from -0.109375 to 0.109375
- b_down: bfloat16 [768], replicated, may hold values from -3 to 3
- cotangent: bfloat16 [128, 2048, 768], P(('dp', 'sub')), may hold values from -6 to 6
Outputs:
- block_out: bfloat16 [128, 2048, 768], P(('dp', 'sub'))
- grad_tokens: bfloat16 [128, 2048, 768], P(('dp', 'sub'))
- grad_router: float32 [768], replicated
- grad_gain_attn: float32 [768], replicated
- grad_qkv: float32 [768, 2304], replicated
- grad_out: float32 [768, 768], replicated
- grad_gain_mlp: float32 [768], replicated
- grad_up: float32 [768, 3072], replicated
- grad_b_up: float32 [3072], replicated
- grad_down: float32 [3072, 768], replicated
- grad_b_down: float32 [768], replicated
Inputs may be any that keep to these rules, and one draw needn't show every extreme that they name: `doc_lengths`: each row's lengths are positive and add up to at most 2048; positions past their sum are padding. `selected`: each row's positions are distinct and ascending.
All inputs are finite; a program needn't handle non-finite values.
Results may differ from a plain program's by a relative error of at most 0.0093.
Values sent between devices are 32-bit elements; how exact they have to be, the bound alone decides.
A program may use at most 256 MiB of HBM per device.

v0:
```python
import jax
import jax.numpy as jnp
from jax import lax
from jax.sharding import PartitionSpec as P

HEADS = 12
HEAD = 64


epsilon = 1e-06


def rms_scale(values):
    return lax.rsqrt(jnp.mean(values * values, axis=-1, keepdims=True) + epsilon)


def pick_rows(table, index):
    return table[index]


def put_rows(table, index, fresh):
    return table.at[index].set(fresh)


def norm_back(d_unit, unit, scale):
    return scale * (d_unit - unit * jnp.mean(d_unit * unit, axis=-1, keepdims=True))


def body(
    tokens,
    doc_lengths,
    selected,
    w_router,
    gain_attn,
    w_qkv,
    w_out,
    gain_mlp,
    w_up,
    b_up,
    w_down,
    b_down,
    cotangent,
):
    row_count = tokens.shape[0]
    chosen = selected.shape[1]
    width = tokens.shape[2]
    doc_ends = jnp.cumsum(doc_lengths, axis=1)
    segment = jnp.sum((selected[:, :, None] >= doc_ends[:, None, :]).astype(jnp.int32), axis=2)
    live_mask = (selected < doc_ends[:, -1:]).astype(jnp.float32)
    live_total = lax.psum(jnp.sum(live_mask), ("dp", "sub"))
    picked = jax.vmap(pick_rows)(tokens, selected).astype(jnp.float32)
    router = jnp.sum(picked * w_router.astype(jnp.float32), axis=-1)
    scale_attn = rms_scale(picked)
    unit_attn = picked * scale_attn
    normed = (unit_attn * gain_attn.astype(jnp.float32)).astype(jnp.bfloat16)
    qkv_rows = jnp.dot(normed, w_qkv, preferred_element_type=jnp.float32).astype(jnp.bfloat16)
    query_rows = qkv_rows[..., :width].reshape(row_count, chosen, HEADS, HEAD)
    key_rows = qkv_rows[..., width : 2 * width].reshape(row_count, chosen, HEADS, HEAD)
    value_rows = qkv_rows[..., 2 * width :].reshape(row_count, chosen, HEADS, HEAD)
    position = jnp.arange(chosen)
    allowed = (position[:, None] >= position[None, :])[None] & (
        segment[:, :, None] == segment[:, None, :]
    )

    def masked_scores():
        raw = (
            jnp.einsum("rqhe,rkhe->rhqk", query_rows, key_rows, preferred_element_type=jnp.float32)
            * 0.125
        )
        return jnp.where(allowed[:, None], raw, -1e30)

    scores = masked_scores()
    row_top = jnp.max(scores, axis=-1, keepdims=True)
    exponent = jnp.exp(scores - row_top)
    row_total = jnp.sum(exponent, axis=-1, keepdims=True)
    attn_probs = exponent / row_total
    log_total = row_top + jnp.log(row_total)
    probs_low = attn_probs.astype(jnp.bfloat16)
    attended = jnp.einsum(
        "rhqk,rkhe->rqhe", probs_low, value_rows, preferred_element_type=jnp.float32
    )
    attended = attended.reshape(row_count, chosen, width).astype(jnp.bfloat16)
    branch = jnp.dot(attended, w_out, preferred_element_type=jnp.float32)
    hidden = picked + router[..., None] * branch
    scale_mlp = rms_scale(hidden)
    unit_mlp = hidden * scale_mlp
    normed_mlp = (unit_mlp * gain_mlp.astype(jnp.float32)).astype(jnp.bfloat16)
    upward = jnp.dot(normed_mlp, w_up, preferred_element_type=jnp.float32) + b_up.astype(
        jnp.float32
    )
    active_full, gelu_back = jax.vjp(jax.nn.gelu, upward)
    active = active_full.astype(jnp.bfloat16)
    result = (
        hidden
        + jnp.dot(active, w_down, preferred_element_type=jnp.float32)
        + b_down.astype(jnp.float32)
    )
    update = (result - picked) * live_mask[..., None]
    block_out = jax.vmap(put_rows)(tokens, selected, (picked + update).astype(jnp.bfloat16))
    cot_picked = jax.vmap(pick_rows)(cotangent, selected).astype(jnp.float32)
    d_result = cot_picked * live_mask[..., None]
    d_mixed = d_result.astype(jnp.bfloat16)
    sum_down = jnp.einsum("rsf,rsd->fd", active, d_mixed, preferred_element_type=jnp.float32)
    sum_b_down = jnp.sum(d_mixed.astype(jnp.float32), axis=(0, 1))
    d_active = jnp.einsum("rsd,fd->rsf", d_mixed, w_down, preferred_element_type=jnp.float32)
    d_upward = gelu_back(d_active)[0].astype(jnp.bfloat16)
    sum_up = jnp.einsum("rsd,rsf->df", normed_mlp, d_upward, preferred_element_type=jnp.float32)
    sum_b_up = jnp.sum(d_upward.astype(jnp.float32), axis=(0, 1))
    d_normed_mlp = jnp.einsum("rsf,df->rsd", d_upward, w_up, preferred_element_type=jnp.float32)
    sum_gain_mlp = jnp.sum(d_normed_mlp * unit_mlp, axis=(0, 1))
    d_hidden = d_result + norm_back(
        d_normed_mlp * gain_mlp.astype(jnp.float32), unit_mlp, scale_mlp
    )
    d_router = jnp.sum(d_hidden * branch, axis=-1)
    d_branch = (router[..., None] * d_hidden).astype(jnp.bfloat16)
    sum_out = jnp.einsum("rsa,rsd->ad", attended, d_branch, preferred_element_type=jnp.float32)
    d_attended = jnp.einsum("rsd,ad->rsa", d_branch, w_out, preferred_element_type=jnp.float32)
    d_attended = d_attended.astype(jnp.bfloat16).reshape(row_count, chosen, HEADS, HEAD)
    again_probs = jnp.exp(masked_scores() - log_total)
    again_low = again_probs.astype(jnp.bfloat16)
    grad_values = jnp.einsum(
        "rhqk,rqhe->rkhe", again_low, d_attended, preferred_element_type=jnp.float32
    )
    d_probs = jnp.einsum(
        "rqhe,rkhe->rhqk", d_attended, value_rows, preferred_element_type=jnp.float32
    )
    d_scores = again_probs * (d_probs - jnp.sum(d_probs * again_probs, axis=-1, keepdims=True))
    d_scores = d_scores.astype(jnp.bfloat16)
    grad_queries = (
        jnp.einsum("rhqk,rkhe->rqhe", d_scores, key_rows, preferred_element_type=jnp.float32)
        * 0.125
    )
    grad_keys = (
        jnp.einsum("rhqk,rqhe->rkhe", d_scores, query_rows, preferred_element_type=jnp.float32)
        * 0.125
    )
    d_qkv = jnp.concatenate(
        [
            grad_queries.reshape(row_count, chosen, width),
            grad_keys.reshape(row_count, chosen, width),
            grad_values.reshape(row_count, chosen, width),
        ],
        axis=-1,
    ).astype(jnp.bfloat16)
    sum_qkv = jnp.einsum("rsd,rsc->dc", normed, d_qkv, preferred_element_type=jnp.float32)
    d_normed = jnp.einsum("rsc,dc->rsd", d_qkv, w_qkv, preferred_element_type=jnp.float32)
    sum_gain_attn = jnp.sum(d_normed * unit_attn, axis=(0, 1))
    d_unit_attn = d_normed * gain_attn.astype(jnp.float32)
    d_picked = (
        d_hidden
        - d_result
        + norm_back(d_unit_attn, unit_attn, scale_attn)
        + d_router[..., None] * w_router.astype(jnp.float32)
    )
    sum_router = jnp.einsum("rs,rsd->d", d_router, picked, precision=lax.Precision.HIGHEST)
    grad_tokens = jax.vmap(put_rows)(
        cotangent, selected, (cot_picked + d_picked).astype(jnp.bfloat16)
    )
    totals = lax.psum(
        (
            sum_router,
            sum_gain_attn,
            sum_qkv,
            sum_out,
            sum_gain_mlp,
            sum_up,
            sum_b_up,
            sum_down,
            sum_b_down,
        ),
        ("dp", "sub"),
    )
    means = [part_sum / live_total for part_sum in totals]
    return (
        block_out,
        grad_tokens,
        means[0],
        means[1],
        means[2],
        means[3],
        means[4],
        means[5],
        means[6],
        means[7],
        means[8],
    )


def solution(mesh):
    placed = (
        P(("dp", "sub"), None, None),
        P(("dp", "sub"), None),
        P(("dp", "sub"), None),
        P(),
        P(),
        P(),
        P(),
        P(),
        P(),
        P(),
        P(),
        P(),
        P(("dp", "sub"), None, None),
    )
    return jax.shard_map(
        body,
        mesh=mesh,
        in_specs=placed,
        out_specs=(
            P(("dp", "sub"), None, None),
            P(("dp", "sub"), None, None),
            P(),
            P(),
            P(),
            P(),
            P(),
            P(),
            P(),
            P(),
            P(),
        ),
        check_vma=False,
    )
```

profile of v0, /device:TPU:0, one launch (start us, length us, event | category | flops | bytes accessed | tf_op | source)
XLA Modules:
  0.0 698.6 jit_solution(6654164218747313658)
XLA Ops:
  7.2 11.2 %copy.94 = bf16[4,2048,768]{2,1,0:T(8,128)(2,1)} copy(bf16[4,2048,768]{2,1,0:T(8,128)(2,1)} %param.13) | data formatting | bytes 25165824
  18.4 2.0 copy-done.9
  20.4 4.8 copy.95
  30.7 20.1 %gather_fusion = bf16[1024,768]{1,0:T(8,128)(2,1)} fusion(bf16[4,2048,768]{2,1,0:T(8,128)(2,1)} %copy.94, s32[1024]{0:T(1024)S(1)} %bitcast.99), kind=kCustom, calls=%fused_computation | custom fusion | bytes 3153920 | tf_op jit(solution)/shard_map/vmap()/gather | solution.py:18
  50.8 2.6 fusion.42
  53.4 6.1 convolution_convert_fusion
  59.4 2.3 fusion.69
  61.7 2.6 copy.60
  64.3 2.6 copy.59
  66.9 2.6 copy.58
  69.5 20.1 %gather_fusion.1 = bf16[1024,768]{1,0:T(8,128)(2,1)} fusion(bf16[4,2048,768]{2,1,0:T(8,128)(2,1)} %copy.95, s32[1024]{0:T(1024)S(1)} %bitcast.100), kind=kCustom, calls=%fused_computation.1 | custom fusion | bytes 3153920 | tf_op jit(solution)/shard_map/vmap()/gather | solution.py:18
  90.7 4.2 fusion.25
  94.9 5.0 fusion.7
  101.3 5.8 fusion.48
  110.1 7.1 %fusion.23 = f32[4,256,3072]{2,1,0:T(8,128)S(1)} fusion(bf16[768,3072]{1,0:T(8,128)(2,1)} %param.21, f32[4,256,768]{2,1,0:T(8,128)S(1)} %get-tuple-element.38, f32[768]{0:T(1024)S(1)} %convert_element_type.95, f32[4,256]{1,0:T(4,128)S(1)} %get-tuple-element.46), kind=kOutput, calls=%fused_computation.47 | convolution fusion | flops 4834197504 | bytes 20454400 | tf_op jit(solution)/shard_map/dot_general | solution.py:88
  117.2 4.6 copy-done.36
  121.8 10.4 %convolution_bitcast_fusion = f32[3072,768]{1,0:T(8,128)} fusion(bf16[4,256,768]{2,1,0:T(8,128)(2,1)S(1)} %bitcast.117, f32[4,256]{1,0:T(4,128)S(1)} %get-tuple-element.28, f32[4,256,3072]{2,1,0:T(8,128)S(1)} %fusion.23, f32[3072]{0:T(1024)S(1)} %copy-done.31), kind=kOutput, calls=%fused_computation.32 | convolution fusion | flops 4865654784 | bytes 23609344 | tf_op jit(solution)/shard_map/rsf,rsd->fd/dot_general | solution.py:103
  132.2 17.0 %convert_reduce_fusion = (f32[3072]{0:T(1024)}, bf16[4,256,3072]{2,1,0:T(8,128)(2,1)}) fusion(f32[4,256,3072]{2,1,0:T(8,128)} %copy-done.36, f32[3072]{0:T(1024)S(1)} %copy-done.31, bf16[3072,768]{1,0:T(8,128)(2,1)} %param.23, bf16[4,256,768]{2,1,0:T(8,128)(2,1)S(1)} %bitcast.118, f32[4,256]{1,0:T(4,128)S(1)} %get-tuple-element.28), kind=kOutput, calls=%fused_computation.13 | convolution fusion | flops 4906546176 | bytes 25194496 | tf_op jit(solution)/shard_map/rsd,fd->rsf/dot_general | solution.py:105
  149.2 9.7 %multiply_reduce_fusion.1 = (f32[768]{0:T(1024)}, f32[4,256]{1,0:T(4,128)S(1)}, f32[4,256,768]{2,1,0:T(8,128)S(1)}) fusion(f32[4,256,768]{2,1,0:T(8,128)S(1)} %get-tuple-element.38, f32[4,256]{1,0:T(4,128)S(1)} %get-tuple-element.46, f32[768]{0:T(1024)S(1)} %convert_element_type.95, bf16[4,256,3072]{2,1,0:T(8,128)(2,1)} %get-tuple-element.45, ...), kind=kOutput, calls=%fused_computation.74 | convolution fusion | flops 4836554752 | bytes 17315840 | tf_op jit(solution)/shard_map/rsf,df->rsd/dot_general | solution.py:109
  158.9 7.8 %convolution_bitcast_fusion.1 = f32[768,3072]{1,0:T(8,128)} fusion(bf16[4,256,3072]{2,1,0:T(8,128)(2,1)S(1)} %copy-done.14, f32[4,256,768]{2,1,0:T(8,128)S(1)} %get-tuple-element.38, f32[768]{0:T(1024)S(1)} %convert_element_type.95, f32[4,256]{1,0:T(4,128)S(1)} %get-tuple-element.46), kind=kOutput, calls=%fused_computation.33 | convolution fusion | flops 4834197504 | bytes 18881536 | tf_op jit(solution)/shard_map/rsd,rsf->df/dot_general | solution.py:107
  168.5 2.9 convolution_bitcast_fusion.3
  171.4 2.6 convolution_convert_fusion.1
  174.0 2.8 copy.63
  176.8 9.3 %fusion.49 = bf16[4,12,64,256]{3,2,1,0:T(8,128)(2,1)} fusion(bf16[4,256,12,64]{1,3,2,0:T(8,128)(2,1)} %bitcast.125, f32[4,12,256]{2,1,0:T(8,128)} %log_add_fusion, f32[4,12,256,256]{2,3,1,0:T(8,128)} %copy-done.1, pred[4,256,256]{1,2,0:T(8,128)(4,1)} %copy-done.12), kind=kOutput, calls=%fused_computation.84 | convolution fusion | flops 416022528 | bytes 16039936 | tf_op jit(solution)/shard_map/rhqk,rqhe->rkhe/dot_general | solution.py:121
  186.1 13.9 %multiply_reduce_fusion = (f32[4,12,256]{2,1,0:T(8,128)S(1)}, f32[4,12,256,256]{2,3,1,0:T(8,128)}) fusion(f32[4,12,256]{2,1,0:T(8,128)S(1)} %copy-done.20, f32[4,12,256,256]{2,3,1,0:T(8,128)} %copy-done.1, pred[4,256,256]{1,2,0:T(8,128)(4,1)S(1)} %copy-done.13, bf16[4,256,12,64]{1,3,2,0:T(8,128)(2,1)} %bitcast.126, bf16[4,256,12,64]{1,3,2,0:T(8,128)(2,1)} %bitcast.123), kind=kOutput, calls=%fused_computation.15 | convolution fusion | flops 418369536 | bytes 28672000 | tf_op jit(solution)/shard_map/rqhe,rkhe->rhqk/dot_general | solution.py:124
  200.0 7.1 %multiply_convert_fusion = bf16[4,12,256,256]{2,3,1,0:T(8,128)(2,1)S(1)} fusion(f32[4,12,256,256]{2,3,1,0:T(8,128)} %get-tuple-element.42, f32[4,12,256]{2,1,0:T(8,128)S(1)} %get-tuple-element.41, f32[4,12,256]{2,1,0:T(8,128)S(1)} %copy-done.20, f32[4,12,256,256]{2,3,1,0:T(8,128)S(1)} %bitcast.102, pred[4,256,256]{1,2,0:T(8,128)(4,1)S(1)} %copy-done.13), kind=kLoop, calls=%fused_computation.14 | loop fusion | flops 18874368 | bytes 31817728 | tf_op jit(solution)/shard_map/convert_element_type | solution.py:128
  207.2 3.2 multiply_convert_fusion.2
  210.4 2.3 multiply_convert_fusion.3
  212.7 2.6 copy.69
  215.3 2.6 copy.67
  217.9 3.0 copy.68
  220.9 9.8 %convolution_bitcast_fusion.2 = f32[768,2304]{1,0:T(8,128)} fusion(bf16[4,256,768]{2,1,0:T(8,128)(2,1)} %copy.69, bf16[4,256,768]{2,1,0:T(8,128)(2,1)} %copy.68, bf16[4,256,768]{2,1,0:T(8,128)(2,1)} %copy.67, bf16[4,256,768]{2,1,0:T(8,128)(2,1)} %bitcast.109, f32[768]{0:T(1024)S(1)} %copy-done.27, f32[4,256]{1,0:T(4,128)} %copy-done.29), kind=kOutput, calls=%fused_computation.35 | convolution fusion | flops 3641180160 | bytes 13376512 | tf_op jit(solution)/shard_map/rsd,rsc->dc/dot_general | solution.py:145
  232.9 13.9 %fusion.45 = bf16[4,256,768]{2,1,0:T(8,128)(2,1)} fusion(bf16[4,256,768]{2,1,0:T(8,128)(2,1)} %bitcast.110, f32[4,256,768]{2,1,0:T(8,128)} %copy-done.2, bf16[3072,768]{1,0:T(8,128)(2,1)} %param.23, f32[4,256]{1,0:T(4,128)S(1)} %get-tuple-element.28, f32[768]{0:T(1024)S(1)} %convert_element_type.99, f32[4,256,3072]{2,1,0:T(8,128)} %copy-done.36, ...), kind=kOutput, calls=%fused_computation.72 | convolution fusion | flops 4868800512 | bytes 23612416 | tf_op jit(solution)/shard_map/dot_general | solution.py:95
  246.8 18.0 %scatter_fusion = bf16[8192,768]{1,0:T(8,128)(2,1)} fusion(bf16[8192,768]{1,0:T(8,128)(2,1)} %bitcast.105, s32[1024]{0:T(1024)S(1)} %bitcast.134, bf16[1024,768]{1,0:T(8,128)(2,1)} %bitcast.131), kind=kCustom, calls=%fused_computation.2 | custom fusion | bytes 4722688
  264.8 7.6 %fusion.41 = (f32[768]{0:T(1024)}, f32[4,256]{1,0:T(4,128)S(1)}, f32[4,256,768]{2,1,0:T(8,128)S(1)}) fusion(f32[4,256]{1,0:T(4,128)} %copy-done.29, bf16[1024,768]{1,0:T(8,128)(2,1)} %gather_fusion, bf16[4,256,768]{2,1,0:T(8,128)(2,1)} %bitcast.111, f32[768]{0:T(1024)} %convert_element_type.87, bf16[768,2304]{1,0:T(8,128)(2,1)S(1)} %copy-done, ...), kind=kOutput, calls=%fused_computation.68 | convolution fusion | flops 3645110528 | bytes 14563328 | tf_op jit(solution)/shard_map/rsc,dc->rsd/dot_general | solution.py:146
  272.4 3.4 convert_reduce_fusion.1
  275.9 18.1 %scatter_fusion.1 = bf16[8192,768]{1,0:T(8,128)(2,1)} fusion(bf16[8192,768]{1,0:T(8,128)(2,1)} %bitcast.103, s32[1024]{0:T(1024)S(1)} %bitcast.135, bf16[1024,768]{1,0:T(8,128)(2,1)} %bitcast.128), kind=kCustom, calls=%fused_computation.3 | custom fusion | bytes 4722688
  294.0 2.1 convolution_reduce_fusion
  296.2 44.6 %all-reduce = (f32[768]{0:T(1024)}, f32[]{:T(128)}, f32[768]{0:T(1024)}, f32[768]{0:T(1024)}, f32[3072]{0:T(1024)}, /*index=5*/f32[768]{0:T(1024)S(1)}) all-reduce(f32[768]{0:T(1024)S(1)} %convolution_reduce_fusion, f32[]{:T(128)} %get-tuple-element.27, f32[768]{0:T(1024)} %get-tuple-element.13, ...), channel_id=1, replica_groups=mesh['dp'=16,'sub'=2] {'dp','sub'}, use_global_device_ids=true, to_apply=%region_13.14 | all-reduce | flops 6145 | bytes 49160 | tf_op jit(solution)/shard_map/psum | solution.py:159
  340.8 1.9 broadcast_divide_fusion.8
  342.7 1.9 broadcast_divide_fusion.7
  344.6 1.9 broadcast_divide_fusion.6
  347.7 1.9 broadcast_divide_fusion.4
  349.7 317.2 %all-reduce.4.cloned.1.call-done = (f32[768,2304]{1,0:T(8,128)}, f32[768,768]{1,0:T(8,128)}, f32[768,3072]{1,0:T(8,128)}, f32[3072,768]{1,0:T(8,128)}) async-done(((f32[768,2304]{1,0:T(8,128)}, f32[768,768]{1,0:T(8,128)}, f32[768,3072]{1,0:T(8,128)}, f32[3072,768]{1,0:T(8,128)}), (f32[768,2304]{1,0:T(8,128)}, f32[768,768]{1,0:T(8,128)}, f32[768,3072]{1,0:T(8,128)}, ...) | async-done | bytes 28311568 | tf_op jit(solution)/shard_map/psum | solution.py:159
  666.9 7.2 %broadcast_divide_fusion.2 = f32[768,2304]{1,0:T(8,128)} fusion(f32[768,2304]{1,0:T(8,128)} %get-tuple-element.23, f32[]{:T(128)} %get-tuple-element.18), kind=kLoop, calls=%fused_computation.60 | loop fusion | flops 1769472 | bytes 14155780 | tf_op jit(solution)/shard_map/div | solution.py:173
  674.1 2.3 broadcast_divide_fusion.3
  676.4 10.1 %broadcast_divide_fusion.1 = f32[768,3072]{1,0:T(8,128)} fusion(f32[768,3072]{1,0:T(8,128)} %get-tuple-element.25, f32[]{:T(128)} %get-tuple-element.18), kind=kLoop, calls=%fused_computation.50 | loop fusion | flops 2359296 | bytes 18874372 | tf_op jit(solution)/shard_map/div | solution.py:173
  686.6 5.0 broadcast_divide_fusion
  (115 shorter events, 16.3 us)
Async XLA Ops:
  7.2 46.2 %copy-start = (bf16[768,2304]{1,0:T(8,128)(2,1)S(1)}, bf16[768,2304]{1,0:T(8,128)(2,1)}, u32[]{:S(2)}) copy-start(bf16[768,2304]{1,0:T(8,128)(2,1)} %param.18) | copy-start | bytes 10616836
  7.2 659.7 %all-reduce.4.cloned.1.call-start = ((), (), s32[]{:S(2)}) async-start(), calls=%async_computation | async-start | bytes 56623104 | tf_op jit(solution)/shard_map/psum | solution.py:159
  7.2 13.2 %copy-start.9 = (bf16[4,2048,768]{2,1,0:T(8,128)(2,1)S(1)}, bf16[4,2048,768]{2,1,0:T(8,128)(2,1)}, u32[]{:S(2)}) copy-start(bf16[4,2048,768]{2,1,0:T(8,128)(2,1)} %param.25) | copy-start | bytes 37748740
  20.4 6.4 copy-start.21
  20.4 7.7 %copy-start.33 = (bf16[768]{0:T(1024)(128)(2,1)S(1)}, bf16[768]{0:T(1024)(128)(2,1)}, u32[]{:S(2)}) copy-start(bf16[768]{0:T(1024)(128)(2,1)} %param.17) | copy-start | bytes 4612
  20.4 8.3 %copy-start.34 = (bf16[768]{0:T(1024)(128)(2,1)S(1)}, bf16[768]{0:T(1024)(128)(2,1)}, u32[]{:S(2)}) copy-start(bf16[768]{0:T(1024)(128)(2,1)} %param.20) | copy-start | bytes 4612
  29.4 21.4 %copy-start.22 = (f32[768]{0:T(1024)}, f32[768]{0:T(1024)S(1)}, u32[]{:S(2)}) copy-start(f32[768]{0:T(1024)S(1)} %convert_element_type.86) | copy-start | bytes 9220
  53.4 6.1 copy-start.29
  69.5 20.1 %copy-start.24 = (s32[4,256]{1,0:T(4,128)S(1)}, s32[4,256]{1,0:T(4,128)}, u32[]{:S(2)}) copy-start(s32[4,256]{1,0:T(4,128)} %convert_reduce_fusion.2) | copy-start | bytes 12292
  90.7 4.2 copy-start.12
  94.8 6.5 copy-start.1
  101.3 5.8 copy-start.3
  101.3 5.8 copy-start.18
  101.3 5.8 copy-start.25
  107.2 1.5 copy-start.16
  108.6 58.1 %copy-start.2 = (f32[4,256,768]{2,1,0:T(8,128)}, f32[4,256,768]{2,1,0:T(8,128)S(1)}, u32[]{:S(2)}) copy-start(f32[4,256,768]{2,1,0:T(8,128)S(1)} %get-tuple-element.38) | copy-start | bytes 9437188
  108.7 0.6 copy-start.35
  110.1 11.7 %copy-start.7 = (bf16[1024,768]{1,0:T(8,128)(2,1)S(1)}, bf16[1024,768]{1,0:T(8,128)(2,1)}, u32[]{:S(2)}) copy-start(bf16[1024,768]{1,0:T(8,128)(2,1)} %gather_fusion.1) | copy-start | bytes 4718596
  110.1 11.7 %copy-start.31 = (f32[3072]{0:T(1024)S(1)}, f32[3072]{0:T(1024)}, u32[]{:S(2)}) copy-start(f32[3072]{0:T(1024)} %convert_element_type.97) | copy-start | bytes 36868
  117.2 4.6 copy-start.36
  149.2 9.7 %copy-start.14 = (bf16[4,256,3072]{2,1,0:T(8,128)(2,1)S(1)}, bf16[4,256,3072]{2,1,0:T(8,128)(2,1)}, u32[]{:S(2)}) copy-start(bf16[4,256,3072]{2,1,0:T(8,128)(2,1)} %get-tuple-element.45) | copy-start | bytes 18874372
  166.7 1.8 copy-start.17
  168.5 3.0 copy-start.10
  168.5 2.9 copy-start.19
  176.8 9.3 %copy-start.13 = (pred[4,256,256]{1,2,0:T(8,128)(4,1)S(1)}, pred[4,256,256]{1,2,0:T(8,128)(4,1)}, u32[]{:S(2)}) copy-start(pred[4,256,256]{1,2,0:T(8,128)(4,1)} %copy-done.12) | copy-start | bytes 786436
  176.8 9.3 %copy-start.20 = (f32[4,12,256]{2,1,0:T(8,128)S(1)}, f32[4,12,256]{2,1,0:T(8,128)}, u32[]{:S(2)}) copy-start(f32[4,12,256]{2,1,0:T(8,128)} %log_add_fusion) | copy-start | bytes 147460
  176.8 23.2 %slice-start = ((s8[12582912]{0:T(1024)(128)(4,1)}), s8[4194304]{0:T(1024)(128)(4,1)S(1)}, s32[]{:S(2)}) async-start(s8[12582912]{0:T(1024)(128)(4,1)} %bitcast.101), calls=%async_computation.1 | async-start | bytes 8388608
  176.8 23.2 %slice-start.1 = ((s8[12582912]{0:T(1024)(128)(4,1)}), s8[4194304]{0:T(1024)(128)(4,1)S(1)}, s32[]{:S(2)}) async-start(s8[12582912]{0:T(1024)(128)(4,1)} %bitcast.101), calls=%async_computation.2 | async-start | bytes 8388608
  186.1 13.9 %slice-start.2 = ((s8[12582912]{0:T(1024)(128)(4,1)}), s8[4194304]{0:T(1024)(128)(4,1)S(1)}, s32[]{:S(2)}) async-start(s8[12582912]{0:T(1024)(128)(4,1)} %bitcast.101), calls=%async_computation.3 | async-start | bytes 8388608
  200.0 7.1 %copy-start.6 = (bf16[4,256,768]{1,2,0:T(8,128)(2,1)S(1)}, bf16[4,256,768]{1,2,0:T(8,128)(2,1)}, u32[]{:S(2)}) copy-start(bf16[4,256,768]{1,2,0:T(8,128)(2,1)} %copy.59) | copy-start | bytes 4718596
  207.1 3.2 copy-start.5
  215.3 5.6 copy-start.27
  264.8 7.6 %copy-start.4 = (bf16[1024,768]{1,0:T(8,128)(2,1)S(1)}, bf16[1024,768]{1,0:T(8,128)(2,1)}, u32[]{:S(2)}) copy-start(bf16[1024,768]{1,0:T(8,128)(2,1)} %gather_fusion) | copy-start | bytes 4718596
  264.8 7.6 %copy-start.8 = (bf16[1024,768]{1,0:T(8,128)(2,1)S(1)}, bf16[1024,768]{1,0:T(8,128)(2,1)}, u32[]{:S(2)}) copy-start(bf16[1024,768]{1,0:T(8,128)(2,1)} %gather_fusion.1) | copy-start | bytes 4718596
  264.8 7.6 %copy-start.11 = (f32[4,256,768]{2,1,0:T(8,128)S(1)}, f32[4,256,768]{2,1,0:T(8,128)}, u32[]{:S(2)}) copy-start(f32[4,256,768]{2,1,0:T(8,128)} %copy-done.10) | copy-start | bytes 9437188
  264.8 7.6 %copy-start.23 = (f32[768]{0:T(1024)S(1)}, f32[768]{0:T(1024)}, u32[]{:S(2)}) copy-start(f32[768]{0:T(1024)} %copy-done.22) | copy-start | bytes 9220
  264.8 7.6 %copy-start.28 = (f32[768]{0:T(1024)S(1)}, f32[768]{0:T(1024)}, u32[]{:S(2)}) copy-start(f32[768]{0:T(1024)} %convert_element_type.87) | copy-start | bytes 9220
  264.8 7.6 %copy-start.30 = (f32[4,256]{1,0:T(4,128)S(1)}, f32[4,256]{1,0:T(4,128)}, u32[]{:S(2)}) copy-start(f32[4,256]{1,0:T(4,128)} %copy-done.29) | copy-start | bytes 12292
  275.9 20.3 %copy-start.26 = (f32[768]{0:T(1024)S(1)}, f32[768]{0:T(1024)}, u32[]{:S(2)}) copy-start(f32[768]{0:T(1024)} %get-tuple-element.34) | copy-start | bytes 9220
  275.9 20.3 %copy-start.32 = (f32[768]{0:T(1024)S(1)}, f32[768]{0:T(1024)}, u32[]{:S(2)}) copy-start(f32[768]{0:T(1024)} %get-tuple-element.11) | copy-start | bytes 9220
  666.9 7.2 %copy-start.15 = (f32[768,768]{1,0:T(8,128)S(1)}, f32[768,768]{1,0:T(8,128)}, u32[]{:S(2)}) copy-start(f32[768,768]{1,0:T(8,128)} %get-tuple-element.24) | copy-start | bytes 7077892
  674.1 12.5 %slice-start.3 = ((s8[9437184]{0:T(1024)(128)(4,1)}), s8[4194304]{0:T(1024)(128)(4,1)S(1)}, s32[]{:S(2)}) async-start(s8[9437184]{0:T(1024)(128)(4,1)} %bitcast.120), calls=%async_computation.4 | async-start | bytes 8388608
  676.4 10.1 %slice-start.4 = ((s8[9437184]{0:T(1024)(128)(4,1)}), s8[4194304]{0:T(1024)(128)(4,1)S(1)}, s32[]{:S(2)}) async-start(s8[9437184]{0:T(1024)(128)(4,1)} %bitcast.120), calls=%async_computation.5 | async-start | bytes 8388608
  676.4 10.1 %slice-start.5 = ((s8[9437184]{0:T(1024)(128)(4,1)}), s8[1048576]{0:T(1024)(128)(4,1)S(1)}, s32[]{:S(2)}) async-start(s8[9437184]{0:T(1024)(128)(4,1)} %bitcast.120), calls=%async_computation.6 | async-start | bytes 2097152
Sparse Core Ops, SparseCore 0:
  230.9 435.9 all-reduce.3
where the time goes:
time: 708 us; the launch traced here: 699 us
  waiting for transfers between devices  317 us (45%)
  matrix products  137 us (19%)
  local copies, waits for them, and re-layouts  121 us (17%)
  other arithmetic  64 us (9%)
  blocking collectives  44.6 us (6%)
  between operations  14.7 us (2%)
    psum x1, waiting for transfers between devices, body(): lax.psum((sum_router, sum_gain_attn, sum_qkv, sum_out, sum_gain_mlp, sum_...  317 us
    unnamed x92, local copies, waits for them, and re-layouts  59.1 us
    psum x1, blocking collectives, body(): lax.psum((sum_router, sum_gain_attn, sum_qkv, sum_out, sum_gain_mlp, sum_...  44.6 us
    gather x2, local copies, waits for them, and re-layouts, pick_rows(): return table[index]  40.2 us
    div x9, other arithmetic, body(): means = [part_sum / live_total for part_sum in totals]  33.5 us
    dot_general x1, matrix products, body(): jnp.einsum('rsd,fd->rsf', d_mixed, w_down, preferred_element_type=jnp.flo...  17 us
  transfers between devices with their start and end apart: 1, of which 1 were waited for; matrix products, arithmetic and copies ran while one was open for 11% of the time, Pallas kernels for 0%

commit v1 on v0

v1 whole, which is shorter than its diff:
```python
import functools

import jax
import jax.numpy as jnp
from jax import lax
from jax.experimental import pallas as pl
from jax.experimental.pallas import tpu as pltpu
from jax.sharding import PartitionSpec as P

HEADS = 12
HEAD = 64
EPS = 1e-06
CHUNK = 2048
GROUP = 3 * CHUNK
PIECE = 512
BIG = -1e30
GELU_A = 0.7978845608028654
GELU_B = 0.044715
ROUNDS = {1: 0, 2: 1, 4: 3}
MESH = pl.DeviceIdType.MESH
F32 = jnp.float32
BF16 = jnp.bfloat16


def nn(a, b):
    return lax.dot_general(a, b, (((1,), (0,)), ((), ())), preferred_element_type=F32)


def nt(a, b):
    return lax.dot_general(a, b, (((1,), (1,)), ((), ())), preferred_element_type=F32)


def tn(a, b):
    return lax.dot_general(a, b, (((0,), (0,)), ((), ())), preferred_element_type=F32)


def lanes(shape):
    return lax.broadcasted_iota(jnp.int32, shape, len(shape) - 1)


def row_mean(v):
    return jnp.mean(v, axis=-1, keepdims=True)


def colsum(v):
    total = jnp.sum(v, axis=0, keepdims=True)
    return jnp.concatenate([total[:, j : j + 128] for j in range(0, v.shape[1], 128)], axis=0)


def when(cond, act):
    if cond is None:
        act()
    else:
        pl.when(cond)(act)


def at8(v):
    return v if isinstance(v, int) else pl.multiple_of(v, 8)


def first_kernel(
    lens, sel_col, sel_row, tokens, cot, w_router, gain_attn, w_qkv, w_out, gain_mlp,
    picked_o, cot_o, dmix_o, normed_o, qkv_o, att_o, cols_o, bias_o, branch_o, nm_o, live_o,
):
    r = pl.program_id(0)
    sel, selr = sel_col[0], sel_row[0]
    chosen = sel.shape[0]
    end = jnp.int32(0)
    seg = jnp.zeros(sel.shape, jnp.int32)
    segr = jnp.zeros(selr.shape, jnp.int32)
    for d in range(lens.shape[1]):
        end = end + lens[r, d]
        seg = seg + (sel >= end).astype(jnp.int32)
        segr = segr + (selr >= end).astype(jnp.int32)
    live = (sel < end).astype(F32)
    count = jnp.broadcast_to(jnp.sum(live), live_o.shape)

    @pl.when(r == 0)
    def _():
        live_o[...] = count

    @pl.when(r > 0)
    def _():
        live_o[...] += count

    spots = tokens.shape[1]
    hot = jnp.where(lanes((chosen, spots)) == sel, 1.0, 0.0).astype(BF16)
    picked = nn(hot, tokens[0])
    cot_rows = nn(hot, cot[0])
    picked_o[...] = picked.astype(BF16)
    cot_o[...] = cot_rows.astype(BF16)
    dmix_o[...] = (cot_rows * live).astype(BF16)
    router = jnp.sum(picked * w_router[...].astype(F32), axis=-1, keepdims=True)
    scale_attn = lax.rsqrt(row_mean(picked * picked) + EPS)
    normed = (picked * scale_attn * gain_attn[...].astype(F32)).astype(BF16)
    normed_o[...] = normed
    qkv_o[...] = nn(normed, w_qkv[...]).astype(BF16)
    width = picked.shape[1]
    causal = lanes((chosen, chosen)) <= lax.broadcasted_iota(jnp.int32, (chosen, chosen), 0)
    bias_o[...] = jnp.where(causal & (seg == segr), 0.0, BIG).astype(BF16)
    lane = lanes((chosen, 128))
    is_low = lane < HEAD
    cols = jnp.zeros((chosen, 128), F32)
    for pair in range(HEADS // 2):
        q = qkv_o[:, pair * 128 : pair * 128 + 128]
        k = qkv_o[:, width + pair * 128 : width + pair * 128 + 128]
        v = qkv_o[:, 2 * width + pair * 128 : 2 * width + pair * 128 + 128]
        outs = []
        for a in range(2):
            keep = jnp.where(is_low if a == 0 else ~is_low, HEAD**-0.5, 0.0).astype(BF16)
            scores = nt(q * keep, k) + bias_o[...].astype(F32)
            top = jnp.max(scores, axis=-1, keepdims=True)
            exponent = jnp.exp(scores - top)
            total = jnp.sum(exponent, axis=-1, keepdims=True)
            outs.append(nn((exponent * (1.0 / total)).astype(BF16), v))
            cols = jnp.where(lane == 2 * pair + a, top + jnp.log(total), cols)
        att_o[:, pair * 128 : pair * 128 + 128] = jnp.where(is_low, outs[0], outs[1]).astype(BF16)
    branch = nn(att_o[...], w_out[...])
    branch_o[...] = branch
    hidden = picked + router * branch
    scale_mlp = lax.rsqrt(row_mean(hidden * hidden) + EPS)
    nm_o[...] = (hidden * scale_mlp * gain_mlp[...].astype(F32)).astype(BF16)
    for at, col in enumerate((router, live, scale_attn, scale_mlp)):
        cols = jnp.where(lane == HEADS + at, col, cols)
    cols_o[...] = cols


def first(tokens, doc_lengths, selected, cotangent, w_router, gain_attn, w_qkv, w_out, gain_mlp):
    rows, spots, width = tokens.shape
    chosen = selected.shape[1]
    n = rows * chosen

    def whole(a):
        return pl.BlockSpec(a.shape, lambda r: (0,) * a.ndim)

    def out(cols, kind):
        return jax.ShapeDtypeStruct((n, cols), kind), pl.BlockSpec((chosen, cols), lambda r: (r, 0))

    outs = [
        out(width, BF16), out(width, BF16), out(width, BF16), out(width, BF16), out(3 * width, BF16),
        out(width, BF16), out(128, F32), out(chosen, BF16), out(width, F32), out(width, BF16),
        (jax.ShapeDtypeStruct((8, 128), F32), pl.BlockSpec((8, 128), lambda r: (0, 0))),
    ]
    return pl.pallas_call(
        first_kernel,
        grid=(rows,),
        in_specs=[
            pl.BlockSpec(memory_space=pltpu.SMEM),
            pl.BlockSpec((1, chosen, 1), lambda r: (r, 0, 0)),
            pl.BlockSpec((1, 1, chosen), lambda r: (r, 0, 0)),
            pl.BlockSpec((1, spots, width), lambda r: (r, 0, 0)),
            pl.BlockSpec((1, spots, width), lambda r: (r, 0, 0)),
            whole(w_router), whole(gain_attn), whole(w_qkv), whole(w_out), whole(gain_mlp),
        ],
        out_specs=[o[1] for o in outs],
        out_shape=[o[0] for o in outs],
        compiler_params=pltpu.CompilerParams(vmem_limit_bytes=50 * 2**20),
    )(
        doc_lengths, selected[:, :, None], selected[:, None, :], tokens, cotangent,
        w_router, gain_attn, w_qkv, w_out, gain_mlp,
    )


class Line:
    def __init__(self, n, q, peer):
        self.n, self.q, self.peer = n, q, peer
        self.rounds = ROUNDS[n]
        if n == 4:
            self.side = q // 2
            self.inner = (q == 1) | (q == 2)
            self.outer = jnp.logical_not(self.inner)

    def rs_send(self, r, size):
        h, s = size // self.n, self.q if self.n == 2 else getattr(self, "side", 0)
        if self.n == 2:
            return None, (1 - s) * h, h, self.peer(1 - s)
        if r == 0:
            return self.outer, (1 - s) * h, 3 * h, self.peer(1 + s)
        if r == 1:
            return self.inner, (1 - s) * 2 * h, 2 * h, self.peer(2 - s)
        return self.inner, s * 3 * h, h, self.peer(3 * s)

    def rs_recv(self, r, size):
        h, s = size // self.n, self.q if self.n == 2 else getattr(self, "side", 0)
        if self.n == 2:
            return None, s * h, h
        if r == 0:
            return self.inner, (1 - s) * h, 3 * h
        if r == 1:
            return self.inner, s * 2 * h, 2 * h
        return self.outer, s * 3 * h, h

    def ag_send(self, r, size):
        h, s = size // self.n, self.q if self.n == 2 else getattr(self, "side", 0)
        if self.n == 2:
            return None, s * h, h, self.peer(1 - s)
        if r == 0:
            return self.outer, s * 3 * h, h, self.peer(1 + s)
        if r == 1:
            return self.inner, s * 2 * h, 2 * h, self.peer(2 - s)
        return self.inner, (1 - s) * h, 3 * h, self.peer(3 * s)

    def ag_recv(self, r, size):
        h, s = size // self.n, self.q if self.n == 2 else getattr(self, "side", 0)
        if self.n == 2:
            return None, (1 - s) * h, h
        if r == 0:
            return self.inner, s * 3 * h, h
        if r == 1:
            return self.inner, (1 - s) * 2 * h, 2 * h
        return self.outer, (1 - s) * h, 3 * h


def recv_rows(sizes, rows):
    total = 0
    for n in sizes:
        rows = rows // n
        total += {1: 0, 2: 1, 4: 5}[n] * rows
    return total


class Part:
    def __init__(self, lines, rows):
        self.steps = []
        base, size, slot = 0, rows, 0
        levels = []
        for ln in lines:
            h = size // ln.n
            offs = {1: [], 2: [slot], 4: [slot, slot + 3 * h, slot]}[ln.n]
            slot += {1: 0, 2: 1, 4: 5}[ln.n] * h
            levels.append((ln, base, size))
            for r in range(ln.rounds):
                self.steps.append(("rs", ln, r, base, size, offs[r]))
            if ln.n > 1:
                base = base + ln.q * h
            size = h
        self.own = (base, size)
        self.n_rs = len(self.steps)
        for ln, b, s in reversed(levels):
            for r in range(ln.rounds):
                self.steps.append(("ag", ln, r, b, s, None))


def lags_of(n_steps):
    lags = [0]
    for k in range(n_steps):
        lags.append(lags[-1] + (2 if k < 2 or k >= n_steps - 2 else 1))
    return lags


def sums_kernel(
    cfg,
    nm_h, dmix_h, normed_h, qkv_h, att_h, cols_h, bias_h, branch_h, picked_h, cot_h, w_up_h, w_down_h, w_qkv_h, w_out_h,
    live_in, b_up, b_down, w_router, gain_attn, gain_mlp,
    sums, small_o, new_block, new_grad,
    nm, nm_t, dmix, w_up, w_down, act, slope, d_up, mixed, d_nm, qkv, att, cols, bias, branch, picked, cot, w_qkv, w_out,
    stage, cbuf, acc, rbuf, vecs, live_s, tiny,
    load_sem, w_sem, row_sem, out_sem, c_send, c_recv, x_send, x_recv, own_sem, f_send, f_recv, t_send, t_recv,
):
    n0, n1, n2 = cfg["dims"]
    lags, n_chunks, n_small = cfg["lags"], cfg["chunks"], cfg["small"]
    n_steps, slots = len(lags) - 1, acc.shape[0]
    dp, sub = lax.axis_index("dp"), lax.axis_index("sub")
    q2, q1, q0 = dp % n2, (dp // n2) % n1, dp // (n2 * n1)

    def chip(a, b, c):
        return (a * (n1 * n2) + b * n2 + c, sub)

    peers = [lambda v: chip(v, q1, q2), lambda v: chip(q0, v, q2), lambda v: chip(q0, q1, v)]
    places = list(zip((n0, n1, n2), (q0, q1, q2), peers, strict=True))
    l0, l1, l2 = (Line(n, q, peer) for n, q, peer in places)
    core = (dp, 1 - sub)
    part_rows = CHUNK // 4
    parts = [Part([l2, l0, l1], part_rows), Part([l1, l0, l2], part_rows)]
    n_rs = parts[0].n_rs
    tokens, width = nm.shape
    chosen = bias.shape[1]
    rows = tokens // chosen
    pieces = w_up_h.shape[1] // PIECE

    loads = [
        pltpu.make_async_copy(src, dst, load_sem.at[i])
        for i, (src, dst) in enumerate(
            (
                (nm_h, nm), (dmix_h, dmix), (qkv_h, qkv), (att_h, att), (cols_h, cols), (bias_h, bias),
                (picked_h, picked), (cot_h, cot), (w_qkv_h, w_qkv), (w_out_h, w_out),
            )
        )
    ]

    def weights_in(f):
        cut = pl.ds(pl.multiple_of(f * PIECE, PIECE), PIECE)
        slot = f % 2
        return (
            pltpu.make_async_copy(w_up_h.at[:, cut], w_up.at[slot], w_sem.at[slot, 0]),
            pltpu.make_async_copy(w_down_h.at[cut], w_down.at[slot], w_sem.at[slot, 1]),
        )

    def branch_in(r):
        return pltpu.make_async_copy(branch_h.at[pl.ds(r * chosen, chosen)], branch.at[r % 2], row_sem.at[r % 2])

    def normed_in():
        return pltpu.make_async_copy(normed_h, nm, load_sem.at[len(loads)])

    for i in range(2):
        loads[i].start()
    for copy in weights_in(0):
        copy.start()

    greeted = [core] + [peer((q + d) % n) for n, q, peer in places for d in range(1, n)]
    barrier = pltpu.get_barrier_semaphore()
    for device in greeted:
        pl.semaphore_signal(barrier, inc=1, device_id=device, device_id_type=MESH)
    mixed[...] = jnp.zeros_like(mixed)
    d_nm[...] = jnp.zeros_like(d_nm)
    for i in range(2):
        loads[i].wait()
    for i in range(2, len(loads)):
        loads[i].start()
    vecs[...] = jnp.zeros_like(vecs)
    for r in range(rows):
        cut = pl.ds(r * chosen, chosen)
        nm_t[:, cut] = nm[cut].T
        vecs[24:30] += colsum(dmix[cut].astype(F32))
    pl.semaphore_wait(barrier, len(greeted))


    def half_out(c):
        j = c % 3
        return pltpu.make_async_remote_copy(
            src_ref=stage.at[pl.ds(at8(j * CHUNK + (1 - sub) * (CHUNK // 2)), CHUNK // 2)], dst_ref=cbuf.at[j],
            send_sem=c_send.at[c], recv_sem=c_recv.at[c], device_id=core, device_id_type=MESH,
        )

    def out_copy(c, p, k):
        kind, ln, r, base, size, slot = parts[p].steps[k]
        who, off, n, device = (ln.rs_send if kind == "rs" else ln.ag_send)(r, size)
        here = pl.ds(at8(p * part_rows + base + off), n)
        if kind == "rs":
            src, dst = acc.at[c % slots, here], rbuf.at[c % slots, p, pl.ds(slot, n)]
        else:
            dst = sums.at[c, sub, here]
            src = acc.at[c % slots, here] if k == n_rs else dst
        return who, pltpu.make_async_remote_copy(
            src_ref=src, dst_ref=dst, send_sem=x_send.at[c, p, k], recv_sem=x_recv.at[c, p, k],
            device_id=device, device_id_type=MESH,
        )

    def own_copy(c, p):
        base, n = parts[p].own
        here = pl.ds(at8(p * part_rows + base), n)
        return pltpu.make_async_copy(acc.at[c % slots, here], sums.at[c, sub, here], own_sem.at[c, p])

    def begin(c, p, k):
        who, copy = out_copy(c, p, k)
        when(who, copy.start)
        if k == n_rs:
            own_copy(c, p).start()

    def finish(c, p, k):
        kind, ln, r, base, size, slot = parts[p].steps[k]
        who, off, n = (ln.rs_recv if kind == "rs" else ln.ag_recv)(r, size)
        here = pl.ds(at8(p * part_rows + base + off), n)
        came = rbuf.at[c % slots, p, pl.ds(slot, n)] if kind == "rs" else sums.at[c, sub, here]

        def take():
            pltpu.make_async_remote_copy(
                src_ref=came, dst_ref=came, send_sem=x_send.at[c, p, k], recv_sem=x_recv.at[c, p, k],
                device_id=core, device_id_type=MESH,
            ).wait_recv()
            if kind == "rs":
                region = acc.at[c % slots, here]
                region[...] = region[...] + came[...]

        when(who, take)
        who, copy = out_copy(c, p, k)
        when(who, copy.wait_send)
        if k == n_rs:
            own_copy(c, p).wait()
        if k == n_rs - 1:
            base, n = parts[p].own
            mine = acc.at[c % slots, pl.ds(at8(p * part_rows + base), n)]
            mine[...] = mine[...] / live_s[0:1]

    def half_back(c, half):
        return pltpu.make_async_remote_copy(
            src_ref=sums.at[c, half], dst_ref=sums.at[c, half], send_sem=f_send.at[c], recv_sem=f_recv.at[c],
            device_id=core, device_id_type=MESH,
        )

    def events(t):
        for k in range(n_steps, -1, -1):
            c = t - 1 - lags[k]

            def event(k=k, c=c):
                for p in range(2):
                    if k > 0:
                        finish(c, p, k - 1)
                    elif p == 0:
                        half_out(c).wait()
                        mine = pl.ds(at8((c % 3) * CHUNK + sub * (CHUNK // 2)), CHUNK // 2)
                        acc[c % slots] = stage[mine] + cbuf[c % 3]
                    if k < n_steps:
                        begin(c, p, k)
                if k == n_steps:
                    half_back(c, sub).start()

            pl.when((c >= 0) & (c < n_chunks))(event)


    pairs = [core]
    for n, q, peer in places:
        bit = 1
        while bit < n:
            pairs.append(peer(q + bit - 2 * bit * ((q // bit) % 2)))
            bit *= 2

    def tiny_copy(which, i):
        here = pl.ds(0, 8) if which == 0 else pl.ds(8, n_small)
        return pltpu.make_async_remote_copy(
            src_ref=tiny.at[0, i, here], dst_ref=tiny.at[1, i, here],
            send_sem=t_send.at[which, i], recv_sem=t_recv.at[which, i], device_id=pairs[i], device_id_type=MESH,
        )

    def tiny_steps(t, first, which, total):
        here = pl.ds(0, 8) if which == 0 else pl.ds(8, n_small)
        for i in range(len(pairs) + 1):

            def step(i=i):
                if i > 0:
                    tiny_copy(which, i - 1).wait()
                    total[...] = total[...] + tiny[1, i - 1, here]
                if i < len(pairs):
                    tiny[0, i, here] = total[...]
                    tiny_copy(which, i).start()
                elif which == 1:
                    small_o[...] = total[...] / live_s[0:1]

            pl.when(t == first + i)(step)


    def put(base, block, value):
        for j in range(value.shape[1] // 128):
            stage[base + j * block : base + (j + 1) * block] = value[:, j * 128 : (j + 1) * 128]

    def piece_up(f):
        for copy in weights_in(f):
            copy.wait()

        def more():
            for copy in weights_in(f + 1):
                copy.start()

        pl.when(f + 1 < pieces)(more)
        slot = f % 2
        b = b_up[:, pl.ds(pl.multiple_of(f * PIECE, PIECE), PIECE)].astype(F32)
        for r in range(rows):
            cut = pl.ds(r * chosen, chosen)
            u = nn(nm[cut], w_up[slot]) + b
            u2 = u * u
            t = jnp.tanh(GELU_A * u * (1.0 + GELU_B * u2))
            act[cut] = (0.5 * u * (1.0 + t)).astype(BF16)
            slope[cut] = 0.5 * (1.0 + t) + 0.5 * u * (1.0 - t * t) * (GELU_A * (1.0 + 3.0 * GELU_B * u2))
        put(0, PIECE, tn(act[...], dmix[...]))

    def piece_back(f):
        slot = f % 2
        sums_b = jnp.zeros((PIECE // 128, 128), F32)
        for r in range(rows):
            cut = pl.ds(r * chosen, chosen)
            d = (nt(dmix[cut], w_down[slot]) * slope[cut]).astype(BF16)
            d_up[cut] = d
            sums_b = sums_b + colsum(d.astype(F32))
        vecs[pl.ds(at8(32 + 8 * f), PIECE // 128)] = sums_b
        put(PIECE * 6, width, nn(nm_t[...], d_up[...]))

    def piece_on(f):
        slot = f % 2
        for r in range(rows):
            cut = pl.ds(r * chosen, chosen)
            mixed[cut] += nn(act[cut], w_down[slot])
            d_nm[cut] += nt(d_up[cut], w_up[slot])


    lane = lanes((chosen, 128))
    is_low = lane < HEAD

    def col(r, at):
        return cols[pl.ds(r * chosen, chosen), at : at + 1]

    def hidden_back():
        for i in range(2, len(loads)):
            loads[i].wait()
        branch_in(0).start()
        for r in range(rows):
            branch_in(r).wait()
            if r + 1 < rows:
                branch_in(r + 1).start()
            cut = pl.ds(r * chosen, chosen)
            br = branch[r % 2]
            x = picked[cut].astype(F32)
            router, live, scale = col(r, HEADS), col(r, HEADS + 1), col(r, HEADS + 3)
            hidden = x + router * br
            unit = hidden * scale
            d_res = dmix[cut].astype(F32)
            dn = d_nm[cut]
            vecs[16:22] += colsum(dn * unit)
            d_unit = dn * gain_mlp[...].astype(F32)
            d_hidden = d_res + scale * (d_unit - unit * row_mean(d_unit * unit))
            dmix[cut] = (x + (hidden + mixed[cut] + b_down[...].astype(F32) - x) * live).astype(BF16)
            d_router = jnp.sum(d_hidden * br, axis=-1, keepdims=True)
            vecs[0:6] += colsum(d_router * x)
            d_branch = (router * d_hidden).astype(BF16)
            nm[cut] = d_branch
            mixed[cut] = d_hidden - d_res + d_router * w_router[...].astype(F32)
        pltpu.make_async_copy(dmix, new_block, out_sem.at[0]).start()
        put(0, width, tn(att[...], nm[...]))
        for r in range(rows):
            cut = pl.ds(r * chosen, chosen)
            att[cut] = nt(nm[cut], w_out[...]).astype(BF16)
        normed_in().start()

    def attention_back(r):
        def one_pair(pair, carry):
            cut = pl.ds(r * chosen, chosen)
            sq = pl.ds(pl.multiple_of(pair * 128, 128), 128)
            sk = pl.ds(pl.multiple_of(width + pair * 128, 128), 128)
            sv = pl.ds(pl.multiple_of(2 * width + pair * 128, 128), 128)
            q, k, v, do = qkv[cut, sq], qkv[cut, sk], qkv[cut, sv], att[cut, sq]
            made = []
            for a in range(2):
                side = is_low if a == 0 else ~is_low
                keep = jnp.where(side, 1.0, 0.0).astype(BF16)
                log_total = jnp.sum(jnp.where(lane == 2 * pair + a, cols[cut], 0.0), axis=-1, keepdims=True)
                probs = jnp.exp(nt(q * keep, k) * HEAD**-0.5 + bias[cut].astype(F32) - log_total)
                d_probs = nt(do * keep, v)
                d_scores = probs * (d_probs - jnp.sum(d_probs * probs, axis=-1, keepdims=True))
                d_scores = d_scores.astype(BF16)
                made.append((nn(d_scores, k), tn(d_scores, q), tn(probs.astype(BF16), do)))
            dq, dk, dv = (jnp.where(is_low, x, y) for x, y in zip(*made, strict=True))
            qkv[cut, sq] = (dq * HEAD**-0.5).astype(BF16)
            qkv[cut, sk] = (dk * HEAD**-0.5).astype(BF16)
            qkv[cut, sv] = dv.astype(BF16)
            return carry

        lax.fori_loop(0, HEADS // 2, one_pair, 0)

    def tokens_back(r):
        cut = pl.ds(r * chosen, chosen)
        d_normed = nt(qkv[cut], w_qkv[...])
        x = picked[cut].astype(F32)
        scale = col(r, HEADS + 2)
        unit = x * scale
        vecs[8:14] += colsum(d_normed * unit)
        d_unit = d_normed * gain_attn[...].astype(F32)
        d_picked = mixed[cut] + scale * (d_unit - unit * row_mean(d_unit * unit))
        cot[cut] = (cot[cut].astype(F32) + d_picked).astype(BF16)

    def compute(t):
        @pl.when(t < 3 * pieces)
        def _():
            f = t // 3
            pl.when(t % 3 == 0)(lambda: piece_up(f))
            pl.when(t % 3 == 1)(lambda: piece_back(f))
            pl.when(t % 3 == 2)(lambda: piece_on(f))

        t0 = 3 * pieces
        pl.when(t == t0)(hidden_back)

        @pl.when(t == t0 + 1)
        def _():
            for r in range(rows // 2):
                attention_back(r)

        @pl.when(t == t0 + 2)
        def _():
            for r in range(rows // 2, rows):
                attention_back(r)
            normed_in().wait()
            put(6 * width, width, tn(nm[...], qkv[:, 0:256]))

        @pl.when(t == t0 + 3)
        def _():
            put(0, width, tn(nm[...], qkv[:, 256:1280]))

        @pl.when(t == t0 + 6)
        def _():
            put(0, width, tn(nm[...], qkv[:, 1280:2304]))

        @pl.when(t == t0 + 8)
        def _():
            for r in range(rows):
                tokens_back(r)
            pltpu.make_async_copy(cot, new_grad, out_sem.at[1]).start()

    live_s[...] = live_in[...]

    def tick(t, carry):
        events(t)
        compute(t)
        pl.when(t < n_chunks)(lambda: half_out(t).start())
        tiny_steps(t, 0, 0, live_s)
        tiny_steps(t, n_chunks, 1, vecs)
        return carry

    lax.fori_loop(0, n_chunks + lags[-1] + 1, tick, 0)

    def last(c, carry):
        half_back(c, sub).wait_send()
        half_back(c, 1 - sub).wait_recv()
        return carry

    lax.fori_loop(0, n_chunks, last, 0)
    pltpu.make_async_copy(dmix, new_block, out_sem.at[0]).wait()
    pltpu.make_async_copy(cot, new_grad, out_sem.at[1]).wait()


def device_sums(mesh, made, weights, vectors):
    picked, cot, dmix, normed, qkv, att, cols, bias, branch, nm, live = made
    w_qkv, w_out, w_up, w_down = weights
    tokens, width = nm.shape
    chosen = bias.shape[1]
    hidden = w_up.shape[1]
    dims = {16: (4, 2, 2), 64: (4, 4, 4)}[mesh.shape["dp"]]
    n_steps = 2 * sum(ROUNDS[n] for n in dims)
    lags = lags_of(n_steps)
    slots = lags[n_steps // 2 + 1] + 1
    chunks = (2 * width * hidden + width * width * 4) // (128 * CHUNK)
    part_rows = CHUNK // 4
    came = max(recv_rows(order, part_rows) for order in ((dims[2], dims[0], dims[1]), (dims[1], dims[0], dims[2])))
    n_tiny = 1 + sum({1: 0, 2: 1, 4: 2}[n] for n in dims)
    n_small = 32 + 8 * (hidden // PIECE)
    vmem, dma = pltpu.VMEM, pltpu.SemaphoreType.DMA
    big = pl.BlockSpec(memory_space=pl.ANY)
    near = pl.BlockSpec(memory_space=vmem)
    return pl.pallas_call(
        functools.partial(sums_kernel, dict(dims=dims, lags=lags, chunks=chunks, small=n_small)),
        in_specs=[big] * 14 + [near] * 6,
        out_specs=[big, near, big, big],
        out_shape=[
            jax.ShapeDtypeStruct((chunks, 2, CHUNK // 2, 128), F32),
            jax.ShapeDtypeStruct((n_small, 128), F32),
            jax.ShapeDtypeStruct((tokens, width), BF16),
            jax.ShapeDtypeStruct((tokens, width), BF16),
        ],
        scratch_shapes=[
            vmem((tokens, width), BF16),
            vmem((width, tokens), BF16),
            vmem((tokens, width), BF16),
            vmem((2, width, PIECE), BF16),
            vmem((2, PIECE, width), BF16),
            vmem((tokens, PIECE), BF16),
            vmem((tokens, PIECE), F32),
            vmem((tokens, PIECE), BF16),
            vmem((tokens, width), F32),
            vmem((tokens, width), F32),
            vmem((tokens, 3 * width), BF16),
            vmem((tokens, width), BF16),
            vmem((tokens, 128), F32),
            vmem((tokens, chosen), BF16),
            vmem((2, chosen, width), F32),
            vmem((tokens, width), BF16),
            vmem((tokens, width), BF16),
            vmem((width, 3 * width), BF16),
            vmem((width, width), BF16),
            vmem((3 * CHUNK, 128), F32),
            vmem((3, CHUNK // 2, 128), F32),
            vmem((slots, CHUNK // 2, 128), F32),
            vmem((slots, 2, came, 128), F32),
            vmem((n_small, 128), F32),
            vmem((8, 128), F32),
            vmem((2, n_tiny, n_small + 8, 128), F32),
            dma((11,)),
            dma((2, 2)),
            dma((2,)),
            dma((2,)),
            dma((chunks,)),
            dma((chunks,)),
            dma((chunks, 2, n_steps)),
            dma((chunks, 2, n_steps)),
            dma((chunks, 2)),
            dma((chunks,)),
            dma((chunks,)),
            dma((2, n_tiny)),
            dma((2, n_tiny)),
        ],
        compiler_params=pltpu.CompilerParams(collective_id=0, has_side_effects=True, vmem_limit_bytes=60 * 2**20),
    )(nm, dmix, normed, qkv, att, cols, bias, branch, picked, cot, w_up, w_down, w_qkv, w_out, live, *vectors)


def last_kernel(
    sel_row, tokens, cot, new_block, new_grad, sums,
    block_out, grad_tokens, grad_qkv, grad_out, grad_up, grad_down, near, in_sems, sems,
):
    step = pl.program_id(0) * pl.num_programs(1) + pl.program_id(1)
    width, hidden = grad_up.shape
    copies = []

    def copy(row, n, dst):
        copies.append((row // GROUP, pltpu.make_async_copy(near.at[pl.ds(row, n)], dst, sems.at[len(copies)])))
        return row + n

    row = 0
    for f in range(0, hidden, PIECE):
        for j in range(0, width, 128):
            row = copy(row, PIECE, grad_down.at[pl.ds(f, PIECE), pl.ds(j, 128)])
        for j in range(f, f + PIECE, 128):
            row = copy(row, width, grad_up.at[:, pl.ds(j, 128)])
    for j in range(0, width, 128):
        row = copy(row, width, grad_out.at[:, pl.ds(j, 128)])
    for j in range(0, 3 * width, 128):
        row = copy(row, width, grad_qkv.at[:, pl.ds(j, 128)])

    groups = sums.shape[0] // GROUP
    fetch = [
        pltpu.make_async_copy(sums.at[pl.ds(g * GROUP, GROUP)], near.at[pl.ds(g * GROUP, GROUP)], in_sems.at[g])
        for g in range(groups)
    ]
    steps = pl.num_programs(0) * pl.num_programs(1)

    @pl.when(step == 0)
    def _():
        for f in fetch:
            f.start()

    for g in range(groups):

        @pl.when(step == jnp.minimum(g, steps - 1))
        def _(g=g):
            fetch[g].wait()
            for at, c in copies:
                if at == g:
                    c.start()

    spots = tokens.shape[1]
    sel = sel_row[0]
    spot = lax.broadcasted_iota(jnp.int32, (spots, sel.shape[1]), 0) + pl.program_id(1) * spots
    hot = jnp.where(spot == sel, 1.0, 0.0)
    hit = jnp.max(hot, axis=-1, keepdims=True) > 0.0
    hot = hot.astype(BF16)
    for old, new, out in ((tokens, new_block, block_out), (cot, new_grad, grad_tokens)):
        fresh = nn(hot, new[...])
        out[0] = jnp.where(hit, fresh, old[0].astype(F32)).astype(BF16)

    @pl.when(step == steps - 1)
    def _():
        for _, c in copies:
            c.wait()


def last(tokens, cotangent, selected, new_block, new_grad, sums, hidden):
    rows, spots, width = tokens.shape
    chosen = selected.shape[1]
    cut = 1024
    big = pl.BlockSpec(memory_space=pl.ANY)
    table = pl.BlockSpec((1, cut, width), lambda r, i: (r, i, 0))
    fresh = pl.BlockSpec((chosen, width), lambda r, i: (r, 0))
    n_copies = hidden // PIECE * (width // 128) + hidden // 128 + 4 * (width // 128)
    return pl.pallas_call(
        last_kernel,
        grid=(rows, spots // cut),
        in_specs=[pl.BlockSpec((1, 1, chosen), lambda r, i: (r, 0, 0)), table, table, fresh, fresh, big],
        out_specs=[table, table, big, big, big, big],
        out_shape=[
            jax.ShapeDtypeStruct(tokens.shape, BF16),
            jax.ShapeDtypeStruct(tokens.shape, BF16),
            jax.ShapeDtypeStruct((width, 3 * width), F32),
            jax.ShapeDtypeStruct((width, width), F32),
            jax.ShapeDtypeStruct((width, hidden), F32),
            jax.ShapeDtypeStruct((hidden, width), F32),
        ],
        scratch_shapes=[
            pltpu.VMEM(sums.shape, F32),
            pltpu.SemaphoreType.DMA((sums.shape[0] // GROUP,)),
            pltpu.SemaphoreType.DMA((n_copies,)),
        ],
        compiler_params=pltpu.CompilerParams(vmem_limit_bytes=50 * 2**20),
    )(selected[:, None, :], tokens, cotangent, new_block, new_grad, sums)


def body(
    mesh, tokens, doc_lengths, selected, w_router, gain_attn, w_qkv, w_out, gain_mlp, w_up, b_up, w_down, b_down, cotangent
):
    hidden = w_up.shape[1]
    w_router, gain_attn, gain_mlp, b_up, b_down = (v[None] for v in (w_router, gain_attn, gain_mlp, b_up, b_down))
    made = first(tokens, doc_lengths, selected, cotangent, w_router, gain_attn, w_qkv, w_out, gain_mlp)
    sums, small, new_block, new_grad = device_sums(
        mesh, made, (w_qkv, w_out, w_up, w_down), (b_up, b_down, w_router, gain_attn, gain_mlp)
    )
    block_out, grad_tokens, grad_qkv, grad_out, grad_up, grad_down = last(
        tokens, cotangent, selected, new_block, new_grad, sums.reshape(-1, 128), hidden
    )
    grad_b_up = small[32:].reshape(-1, 8, 128)[:, : PIECE // 128].reshape(-1)
    grad_router, grad_gain_attn, grad_gain_mlp, grad_b_down = (small[i : i + 6].reshape(-1) for i in (0, 8, 16, 24))
    return (
        block_out,
        grad_tokens,
        grad_router,
        grad_gain_attn,
        grad_qkv,
        grad_out,
        grad_gain_mlp,
        grad_up,
        grad_b_up,
        grad_down,
        grad_b_down,
    )


def solution(mesh):
    split, copied = P(("dp", "sub")), P()
    return jax.shard_map(
        functools.partial(body, mesh),
        mesh=mesh,
        in_specs=(split,) * 3 + (copied,) * 9 + (split,),
        out_specs=(split,) * 2 + (copied,) * 9,
        check_vma=False,
    )
```

time: 708 us -> 324 us (0.46); the launches traced: 699 us -> 323 us
  waiting for transfers between devices: 317 us -> 0 us
  Pallas kernels: 0 us -> 306 us
  matrix products: 137 us -> 0 us
  local copies, waits for them, and re-layouts: 121 us -> 15.8 us
  other arithmetic: 64 us -> 0 us
  blocking collectives: 44.6 us -> 0 us
  between operations: 14.7 us -> 0.9 us
    psum x1 -> x0, waiting for transfers between devices: 317 us -> none  [body(): lax.psum((sum_router, sum_gain_attn, sum_qkv, sum_out, sum_gain_mlp, sum_...]
    pallas_call x0 -> x3, Pallas kernels: none -> 306 us  [the longest x1 242 us: device_sums(): pl.pallas_call(functools.partial(sums_kernel, dict(dims=dims, lags=lags,...]
    dot_general x19 -> x0, matrix products: 137 us -> none  [the longest x1 17 us: body(): jnp.einsum('rsd,fd->rsf', d_mixed, w_down, preferred_element_type=jnp.flo...]
    unnamed x92 -> x20, local copies, waits for them, and re-layouts: 59.1 us -> 6.97 us
    psum x1 -> x0, blocking collectives: 44.6 us -> none  [body(): lax.psum((sum_router, sum_gain_attn, sum_qkv, sum_out, sum_gain_mlp, sum_...]
    gather x2 -> x0, local copies, waits for them, and re-layouts: 40.2 us -> none  [pick_rows(): return table[index]]
    div x11 -> x0, other arithmetic: 33.5 us -> none  [the longest x9 33.5 us: body(): means = [part_sum / live_total for part_sum in totals]]
    reduce_sum x7 -> x0, other arithmetic: 14.6 us -> none  [the longest x1 5 us: body(): row_total = jnp.sum(exponent, axis=-1, keepdims=True)]
  transfers between devices with their start and end apart: 1 -> 0, of which waited for: 1 -> 0; matrix products, arithmetic and copies ran while one was open for 11% -> 0% of each run, Pallas kernels for 0% -> 0%
where the time goes in v1:
time: 324 us; the launch traced here: 323 us
  Pallas kernels  306 us (94%)
  local copies, waits for them, and re-layouts  15.8 us (5%)
    pallas_call x1, Pallas kernels, device_sums(): pl.pallas_call(functools.partial(sums_kernel, dict(dims=dims, lags=lags,...  242 us
    pallas_call x1, Pallas kernels, last(): pl.pallas_call(last_kernel, grid=(rows, spots // cut), in_specs=[pl.Block...  36.2 us
    pallas_call x1, Pallas kernels, first(): pl.pallas_call(first_kernel, grid=(rows,), in_specs=[pl.BlockSpec(memory_...  27.6 us
    unnamed x20, local copies, waits for them, and re-layouts  6.97 us

profile of v1, /device:TPU:0, one launch (start us, length us, event | category | flops | bytes accessed | tf_op | source)
XLA Modules:
  0.0 322.8 jit_solution(7239744459723908142)
XLA Ops:
  0.6 0.7 broadcast_in_dim.24.w_router
  1.3 0.0 copy-start.5
  1.3 0.7 broadcast_in_dim.25.gain_attn
  2.0 0.0 copy-start.6
  2.0 0.7 broadcast_in_dim.26.gain_mlp
  2.7 0.0 copy-start.7
  2.7 1.3 broadcast_in_dim.28.b_down
  4.0 0.7 broadcast_in_dim.22.sel_row
  4.7 1.3 broadcast_in_dim.27.b_up
  6.0 0.9 copy.24.sel_col
  6.9 0.0 copy-start
  6.9 1.3 copy-done
  8.1 0.0 copy-start.9
  8.2 0.7 copy-done.9
  8.8 27.6 %shard_map.212 = (bf16[1024,768]{1,0:T(8,128)(2,1)}, bf16[1024,768]{1,0:T(8,128)(2,1)}, bf16[1024,768]{1,0:T(8,128)(2,1)}, bf16[1024,768]{1,0:T(8,128)(2,1)}, bf...) custom-call(s32[4,16]{1,0:T(4,128)S(1)} %copy-done.9, ...), custom_call_target="tpu_custom_call" | custom-call | tf_op jit(solution)/shard_map/pallas_call | solution.py:144
  36.5 0.0 copy-done.5
  36.5 0.0 copy-done.6
  36.5 0.0 copy-done.7
  36.5 0.0 copy-start.3
  36.5 0.8 copy-done.3
  37.3 0.0 copy-start.4
  37.3 0.8 copy-done.4
  38.1 0.0 copy-start.8
  38.1 0.6 copy-done.8
  38.7 242.2 %shard_map.213 = (f32[27,2,1024,128]{3,2,1,0:T(8,128)}, f32[80,128]{1,0:T(8,128)}, bf16[1024,768]{1,0:T(8,128)(2,1)}, bf16[1024,768]{1,0:T(8,128)(2,1)}) custom-call(bf16[1024,768]{1,0:T(8,128)(2,1)} %get-tuple-element.32.nm_h, bf16[1024,768]{1,0:T(8,128)(2,1)} %get-tuple-element.33.dmix_h, bf16[1024,768]{1,0:T(8,128)(2,1)} %get-tuple-element.34.normed_h, ...), custom_call_target="tpu_custom_call" | custom-call | tf_op jit(solution)/shard_map/pallas_call | solution.py:636
  280.9 1.3 slice_bitcast_fusion.1
  282.2 0.7 slice_bitcast_fusion
  283.0 0.6 slice.24
  283.6 0.0 copy-start.1
  283.6 1.4 copy-done.1
  285.0 0.0 copy-start.2
  285.0 1.4 copy-done.2
  286.4 36.2 %shard_map.214 = (bf16[4,2048,768]{2,1,0:T(8,128)(2,1)}, bf16[4,2048,768]{2,1,0:T(8,128)(2,1)}, f32[768,2304]{1,0:T(8,128)}, f32[768,768]{1,0:T(8,128)}, f32[768,3072]{1,0:T(8,128)}, /*index=5*/f32[3072,768]{1,0:T(8,128)}) custom-call(s32[4,1,256]{2,1,0:T(1,128)S(1)} %broadcast_in_dim.22.sel_row, bf16[4,2048,768]{2,1,0:T(8,128)(2,1)} %tokens.3, ...), custom_call_target="tpu_custom_call" | custom-call | tf_op jit(solution)/shard_map/pallas_call | solution.py:759
Async XLA Ops:
  1.3 35.1 %copy-start.5 = (bf16[1,768]{1,0:T(2,128)(2,1)}, bf16[1,768]{1,0:T(2,128)(2,1)S(1)}, u32[]{:S(2)}) copy-start(bf16[1,768]{1,0:T(2,128)(2,1)S(1)} %broadcast_in_dim.24.w_router) | copy-start | bytes 4612
  2.0 34.4 %copy-start.6 = (bf16[1,768]{1,0:T(2,128)(2,1)}, bf16[1,768]{1,0:T(2,128)(2,1)S(1)}, u32[]{:S(2)}) copy-start(bf16[1,768]{1,0:T(2,128)(2,1)S(1)} %broadcast_in_dim.25.gain_attn) | copy-start | bytes 4612
  2.7 33.8 %copy-start.7 = (bf16[1,768]{1,0:T(2,128)(2,1)}, bf16[1,768]{1,0:T(2,128)(2,1)S(1)}, u32[]{:S(2)}) copy-start(bf16[1,768]{1,0:T(2,128)(2,1)S(1)} %broadcast_in_dim.26.gain_mlp) | copy-start | bytes 4612
  6.9 1.3 copy-start
  8.1 0.7 copy-start.9
  36.5 0.8 copy-start.3
  37.3 0.8 copy-start.4
  38.1 0.6 copy-start.8
  283.6 1.4 copy-start.1
  285.0 1.4 copy-start.2

commit v2 on v1

--- a/solution.py
+++ b/solution.py
@@ -34,6 +34,10 @@
     return lax.dot_general(a, b, (((0,), (0,)), ((), ())), preferred_element_type=F32)
 
 
+def vector(ref):
+    return ref[...].astype(F32)[None]
+
+
 def lanes(shape):
     return lax.broadcasted_iota(jnp.int32, shape, len(shape) - 1)
 
@@ -59,12 +63,14 @@
 
 
 def first_kernel(
-    lens, sel_col, sel_row, tokens, cot, w_router, gain_attn, w_qkv, w_out, gain_mlp,
+    lens, selected, tokens, cot, w_router, gain_attn, w_qkv, w_out, gain_mlp,
     picked_o, cot_o, dmix_o, normed_o, qkv_o, att_o, cols_o, bias_o, branch_o, nm_o, live_o,
 ):
     r = pl.program_id(0)
-    sel, selr = sel_col[0], sel_row[0]
-    chosen = sel.shape[0]
+    chosen = selected.shape[1]
+    selr = selected[pl.ds(r, 1)]
+    diagonal = lanes((chosen, chosen)) == lax.broadcasted_iota(jnp.int32, (chosen, chosen), 0)
+    sel = jnp.sum(jnp.where(diagonal, selr.astype(F32), 0.0), axis=-1, keepdims=True).astype(jnp.int32)
     end = jnp.int32(0)
     seg = jnp.zeros(sel.shape, jnp.int32)
     segr = jnp.zeros(selr.shape, jnp.int32)
@@ -90,9 +96,9 @@
     picked_o[...] = picked.astype(BF16)
     cot_o[...] = cot_rows.astype(BF16)
     dmix_o[...] = (cot_rows * live).astype(BF16)
-    router = jnp.sum(picked * w_router[...].astype(F32), axis=-1, keepdims=True)
+    router = jnp.sum(picked * vector(w_router), axis=-1, keepdims=True)
     scale_attn = lax.rsqrt(row_mean(picked * picked) + EPS)
-    normed = (picked * scale_attn * gain_attn[...].astype(F32)).astype(BF16)
+    normed = (picked * scale_attn * vector(gain_attn)).astype(BF16)
     normed_o[...] = normed
     qkv_o[...] = nn(normed, w_qkv[...]).astype(BF16)
     width = picked.shape[1]
@@ -119,7 +125,7 @@
     branch_o[...] = branch
     hidden = picked + router * branch
     scale_mlp = lax.rsqrt(row_mean(hidden * hidden) + EPS)
-    nm_o[...] = (hidden * scale_mlp * gain_mlp[...].astype(F32)).astype(BF16)
+    nm_o[...] = (hidden * scale_mlp * vector(gain_mlp)).astype(BF16)
     for at, col in enumerate((router, live, scale_attn, scale_mlp)):
         cols = jnp.where(lane == HEADS + at, col, cols)
     cols_o[...] = cols
@@ -146,17 +152,16 @@
         grid=(rows,),
         in_specs=[
             pl.BlockSpec(memory_space=pltpu.SMEM),
-            pl.BlockSpec((1, chosen, 1), lambda r: (r, 0, 0)),
-            pl.BlockSpec((1, 1, chosen), lambda r: (r, 0, 0)),
+            whole(selected),
             pl.BlockSpec((1, spots, width), lambda r: (r, 0, 0)),
             pl.BlockSpec((1, spots, width), lambda r: (r, 0, 0)),
             whole(w_router), whole(gain_attn), whole(w_qkv), whole(w_out), whole(gain_mlp),
         ],
         out_specs=[o[1] for o in outs],
         out_shape=[o[0] for o in outs],
-        compiler_params=pltpu.CompilerParams(vmem_limit_bytes=50 * 2**20),
+        compiler_params=pltpu.CompilerParams(vmem_limit_bytes=63 * 2**20),
     )(
-        doc_lengths, selected[:, :, None], selected[:, None, :], tokens, cotangent,
+        doc_lengths, selected, tokens, cotangent,
         w_router, gain_attn, w_qkv, w_out, gain_mlp,
     )
 
@@ -329,7 +334,7 @@
         j = c % 3
         return pltpu.make_async_remote_copy(
             src_ref=stage.at[pl.ds(at8(j * CHUNK + (1 - sub) * (CHUNK // 2)), CHUNK // 2)], dst_ref=cbuf.at[j],
-            send_sem=c_send.at[c], recv_sem=c_recv.at[c], device_id=core, device_id_type=MESH,
+            send_sem=c_send.at[j], recv_sem=c_recv.at[j], device_id=core, device_id_type=MESH,
         )
 
     def out_copy(c, p, k):
@@ -342,14 +347,14 @@
             dst = sums.at[c, sub, here]
             src = acc.at[c % slots, here] if k == n_rs else dst
         return who, pltpu.make_async_remote_copy(
-            src_ref=src, dst_ref=dst, send_sem=x_send.at[c, p, k], recv_sem=x_recv.at[c, p, k],
+            src_ref=src, dst_ref=dst, send_sem=x_send.at[c % slots, p, k], recv_sem=x_recv.at[c % slots, p, k],
             device_id=device, device_id_type=MESH,
         )
 
     def own_copy(c, p):
         base, n = parts[p].own
         here = pl.ds(at8(p * part_rows + base), n)
-        return pltpu.make_async_copy(acc.at[c % slots, here], sums.at[c, sub, here], own_sem.at[c, p])
+        return pltpu.make_async_copy(acc.at[c % slots, here], sums.at[c, sub, here], own_sem.at[c % slots, p])
 
     def begin(c, p, k):
         who, copy = out_copy(c, p, k)
@@ -365,7 +370,7 @@
 
         def take():
             pltpu.make_async_remote_copy(
-                src_ref=came, dst_ref=came, send_sem=x_send.at[c, p, k], recv_sem=x_recv.at[c, p, k],
+                src_ref=came, dst_ref=came, send_sem=x_send.at[c % slots, p, k], recv_sem=x_recv.at[c % slots, p, k],
                 device_id=core, device_id_type=MESH,
             ).wait_recv()
             if kind == "rs":
@@ -453,7 +458,7 @@
 
         pl.when(f + 1 < pieces)(more)
         slot = f % 2
-        b = b_up[:, pl.ds(pl.multiple_of(f * PIECE, PIECE), PIECE)].astype(F32)
+        b = b_up[pl.ds(pl.multiple_of(f * PIECE, PIECE), PIECE)].astype(F32)[None]
         for r in range(rows):
             cut = pl.ds(r * chosen, chosen)
             u = nn(nm[cut], w_up[slot]) + b
@@ -505,14 +510,14 @@
             d_res = dmix[cut].astype(F32)
             dn = d_nm[cut]
             vecs[16:22] += colsum(dn * unit)
-            d_unit = dn * gain_mlp[...].astype(F32)
+            d_unit = dn * vector(gain_mlp)
             d_hidden = d_res + scale * (d_unit - unit * row_mean(d_unit * unit))
-            dmix[cut] = (x + (hidden + mixed[cut] + b_down[...].astype(F32) - x) * live).astype(BF16)
+            dmix[cut] = (x + (hidden + mixed[cut] + vector(b_down) - x) * live).astype(BF16)
             d_router = jnp.sum(d_hidden * br, axis=-1, keepdims=True)
             vecs[0:6] += colsum(d_router * x)
             d_branch = (router * d_hidden).astype(BF16)
             nm[cut] = d_branch
-            mixed[cut] = d_hidden - d_res + d_router * w_router[...].astype(F32)
+            mixed[cut] = d_hidden - d_res + d_router * vector(w_router)
         pltpu.make_async_copy(dmix, new_block, out_sem.at[0]).start()
         put(0, width, tn(att[...], nm[...]))
         for r in range(rows):
@@ -521,19 +526,18 @@
         normed_in().start()
 
     def attention_back(r):
-        def one_pair(pair, carry):
-            cut = pl.ds(r * chosen, chosen)
-            sq = pl.ds(pl.multiple_of(pair * 128, 128), 128)
-            sk = pl.ds(pl.multiple_of(width + pair * 128, 128), 128)
-            sv = pl.ds(pl.multiple_of(2 * width + pair * 128, 128), 128)
+        cut = pl.ds(pl.multiple_of(r * chosen, chosen), chosen)
+        sides = [jnp.where(side, 1.0, 0.0).astype(BF16) for side in (is_low, ~is_low)]
+        for pair in range(HEADS // 2):
+            sq, sk, sv = (pl.ds(i * width + pair * 128, 128) for i in range(3))
             q, k, v, do = qkv[cut, sq], qkv[cut, sk], qkv[cut, sv], att[cut, sq]
+            scores = [nt(q * side, k) for side in sides]
+            d_values = [nt(do * side, v) for side in sides]
             made = []
             for a in range(2):
-                side = is_low if a == 0 else ~is_low
-                keep = jnp.where(side, 1.0, 0.0).astype(BF16)
-                log_total = jnp.sum(jnp.where(lane == 2 * pair + a, cols[cut], 0.0), axis=-1, keepdims=True)
-                probs = jnp.exp(nt(q * keep, k) * HEAD**-0.5 + bias[cut].astype(F32) - log_total)
-                d_probs = nt(do * keep, v)
+                log_total = cols[cut, 2 * pair + a : 2 * pair + a + 1]
+                probs = jnp.exp(scores[a] * HEAD**-0.5 + bias[cut].astype(F32) - log_total)
+                d_probs = d_values[a]
                 d_scores = probs * (d_probs - jnp.sum(d_probs * probs, axis=-1, keepdims=True))
                 d_scores = d_scores.astype(BF16)
                 made.append((nn(d_scores, k), tn(d_scores, q), tn(probs.astype(BF16), do)))
@@ -541,9 +545,6 @@
             qkv[cut, sq] = (dq * HEAD**-0.5).astype(BF16)
             qkv[cut, sk] = (dk * HEAD**-0.5).astype(BF16)
             qkv[cut, sv] = dv.astype(BF16)
-            return carry
-
-        lax.fori_loop(0, HEADS // 2, one_pair, 0)
 
     def tokens_back(r):
         cut = pl.ds(r * chosen, chosen)
@@ -552,7 +553,7 @@
         scale = col(r, HEADS + 2)
         unit = x * scale
         vecs[8:14] += colsum(d_normed * unit)
-        d_unit = d_normed * gain_attn[...].astype(F32)
+        d_unit = d_normed * vector(gain_attn)
         d_picked = mixed[cut] + scale * (d_unit - unit * row_mean(d_unit * unit))
         cot[cut] = (cot[cut].astype(F32) + d_picked).astype(BF16)
 
@@ -569,13 +570,11 @@
 
         @pl.when(t == t0 + 1)
         def _():
-            for r in range(rows // 2):
-                attention_back(r)
+            lax.fori_loop(0, rows // 2, lambda r, i: (attention_back(r), i)[1], 0)
 
         @pl.when(t == t0 + 2)
         def _():
-            for r in range(rows // 2, rows):
-                attention_back(r)
+            lax.fori_loop(rows // 2, rows, lambda r, i: (attention_back(r), i)[1], 0)
             normed_in().wait()
             put(6 * width, width, tn(nm[...], qkv[:, 0:256]))
 
@@ -674,22 +673,22 @@
             dma((2, 2)),
             dma((2,)),
             dma((2,)),
-            dma((chunks,)),
-            dma((chunks,)),
-            dma((chunks, 2, n_steps)),
-            dma((chunks, 2, n_steps)),
-            dma((chunks, 2)),
+            dma((3,)),
+            dma((3,)),
+            dma((slots, 2, n_steps)),
+            dma((slots, 2, n_steps)),
+            dma((slots, 2)),
             dma((chunks,)),
             dma((chunks,)),
             dma((2, n_tiny)),
             dma((2, n_tiny)),
         ],
-        compiler_params=pltpu.CompilerParams(collective_id=0, has_side_effects=True, vmem_limit_bytes=60 * 2**20),
+        compiler_params=pltpu.CompilerParams(collective_id=0, has_side_effects=True, vmem_limit_bytes=63 * 2**20),
     )(nm, dmix, normed, qkv, att, cols, bias, branch, picked, cot, w_up, w_down, w_qkv, w_out, live, *vectors)
 
 
 def last_kernel(
-    sel_row, tokens, cot, new_block, new_grad, sums,
+    selected, tokens, cot, new_block, new_grad, sums,
     block_out, grad_tokens, grad_qkv, grad_out, grad_up, grad_down, near, in_sems, sems,
 ):
     step = pl.program_id(0) * pl.num_programs(1) + pl.program_id(1)
@@ -733,7 +732,7 @@
                     c.start()
 
     spots = tokens.shape[1]
-    sel = sel_row[0]
+    sel = selected[pl.ds(pl.program_id(0), 1)]
     spot = lax.broadcasted_iota(jnp.int32, (spots, sel.shape[1]), 0) + pl.program_id(1) * spots
     hot = jnp.where(spot == sel, 1.0, 0.0)
     hit = jnp.max(hot, axis=-1, keepdims=True) > 0.0
@@ -759,7 +758,7 @@
     return pl.pallas_call(
         last_kernel,
         grid=(rows, spots // cut),
-        in_specs=[pl.BlockSpec((1, 1, chosen), lambda r, i: (r, 0, 0)), table, table, fresh, fresh, big],
+        in_specs=[pl.BlockSpec(selected.shape, lambda r, i: (0, 0)), table, table, fresh, fresh, big],
         out_specs=[table, table, big, big, big, big],
         out_shape=[
             jax.ShapeDtypeStruct(tokens.shape, BF16),
@@ -774,15 +773,14 @@
             pltpu.SemaphoreType.DMA((sums.shape[0] // GROUP,)),
             pltpu.SemaphoreType.DMA((n_copies,)),
         ],
-        compiler_params=pltpu.CompilerParams(vmem_limit_bytes=50 * 2**20),
-    )(selected[:, None, :], tokens, cotangent, new_block, new_grad, sums)
+        compiler_params=pltpu.CompilerParams(vmem_limit_bytes=63 * 2**20),
+    )(selected, tokens, cotangent, new_block, new_grad, sums)
 
 
 def body(
     mesh, tokens, doc_lengths, selected, w_router, gain_attn, w_qkv, w_out, gain_mlp, w_up, b_up, w_down, b_down, cotangent
 ):
     hidden = w_up.shape[1]
-    w_router, gain_attn, gain_mlp, b_up, b_down = (v[None] for v in (w_router, gain_attn, gain_mlp, b_up, b_down))
     made = first(tokens, doc_lengths, selected, cotangent, w_router, gain_attn, w_qkv, w_out, gain_mlp)
     sums, small, new_block, new_grad = device_sums(
         mesh, made, (w_qkv, w_out, w_up, w_down), (b_up, b_down, w_router, gain_attn, gain_mlp)

time: 324 us -> 296 us (0.914)
  local copies, waits for them, and re-layouts: 15.8 us -> 2.65 us
  Pallas kernels: 306 us -> 293 us
    pallas_call x1, Pallas kernels: 242 us -> 227 us  [device_sums(): pl.pallas_call(functools.partial(sums_kernel, dict(dims=dims, lags=lags,...]
    unnamed x20 -> x0, local copies, waits for them, and re-layouts: 6.97 us -> none
    broadcast_in_dim x7 -> x0, local copies, waits for them, and re-layouts: 6.21 us -> none  [the longest x5 4.62 us: body(): v[None]]
where the time goes in v2:
time: 296 us
  Pallas kernels  293 us (99%)
    pallas_call x1, Pallas kernels, device_sums(): pl.pallas_call(functools.partial(sums_kernel, dict(dims=dims, lags=lags,...  227 us
    pallas_call x1, Pallas kernels, last(): pl.pallas_call(last_kernel, grid=(rows, spots // cut), in_specs=[pl.Block...  37.5 us
    pallas_call x1, Pallas kernels, first(): pl.pallas_call(first_kernel, grid=(rows,), in_specs=[pl.BlockSpec(memory_...  28.3 us

profile of v2, /device:TPU:0, one launch (start us, length us, event | category | flops | bytes accessed | tf_op | source)
XLA Modules:
  0.0 296.1 jit_solution(16619615936711353018)
XLA Ops:
  0.6 28.3 %shard_map.212 = (bf16[1024,768]{1,0:T(8,128)(2,1)}, bf16[1024,768]{1,0:T(8,128)(2,1)}, bf16[1024,768]{1,0:T(8,128)(2,1)}, bf16[1024,768]{1,0:T(8,128)(2,1)}, bf...) custom-call(s32[4,16]{1,0:T(4,128)} %lens.1, ...), custom_call_target="tpu_custom_call" | custom-call | tf_op jit(solution)/shard_map/pallas_call | solution.py:150
  28.9 226.8 %shard_map.213 = (f32[27,2,1024,128]{3,2,1,0:T(8,128)}, f32[80,128]{1,0:T(8,128)}, bf16[1024,768]{1,0:T(8,128)(2,1)}, bf16[1024,768]{1,0:T(8,128)(2,1)}) custom-call(bf16[1024,768]{1,0:T(8,128)(2,1)} %get-tuple-element.32.nm_h, bf16[1024,768]{1,0:T(8,128)(2,1)} %get-tuple-element.33.dmix_h, bf16[1024,768]{1,0:T(8,128)(2,1)} %get-tuple-element.34.normed_h, ...), custom_call_target="tpu_custom_call" | custom-call | tf_op jit(solution)/shard_map/pallas_call | solution.py:635
  255.7 1.3 slice_bitcast_fusion.1
  257.0 0.7 slice_bitcast_fusion
  257.8 0.6 slice.24
  258.4 37.5 %shard_map.214 = (bf16[4,2048,768]{2,1,0:T(8,128)(2,1)}, bf16[4,2048,768]{2,1,0:T(8,128)(2,1)}, f32[768,2304]{1,0:T(8,128)}, f32[768,768]{1,0:T(8,128)}, f32[768,3072]{1,0:T(8,128)}, /*index=5*/f32[3072,768]{1,0:T(8,128)}) custom-call(s32[4,256]{1,0:T(4,128)} %selected.3, bf16[4,2048,768]{2,1,0:T(8,128)(2,1)} %tokens.3, bf16[4,2048,768]{2,1,0:T(8,128)(2,1)} %cot.3, ...), custom_call_target="tpu_custom_call" | custom-call | tf_op jit(solution)/shard_map/pallas_call | solution.py:758

commit v3 on v2

--- a/solution.py
+++ b/solution.py
@@ -688,8 +688,9 @@
 
 
 def last_kernel(
-    selected, tokens, cot, new_block, new_grad, sums,
-    block_out, grad_tokens, grad_qkv, grad_out, grad_up, grad_down, near, in_sems, sems,
+    selected, tokens, cot, new_block, new_grad, small, sums,
+    block_out, grad_tokens, grad_qkv, grad_out, grad_up, grad_down,
+    grad_router, grad_gain_attn, grad_gain_mlp, grad_b_down, grad_b_up, near, in_sems, sems,
 ):
     step = pl.program_id(0) * pl.num_programs(1) + pl.program_id(1)
     width, hidden = grad_up.shape
@@ -721,6 +722,11 @@
     def _():
         for f in fetch:
             f.start()
+        for at, out in ((0, grad_router), (8, grad_gain_attn), (16, grad_gain_mlp), (24, grad_b_down)):
+            for j in range(width // 128):
+                out[j * 128 : (j + 1) * 128] = small[at + j]
+        for j in range(hidden // 128):
+            grad_b_up[j * 128 : (j + 1) * 128] = small[32 + 8 * (j * 128 // PIECE) + j % (PIECE // 128)]
 
     for g in range(groups):
 
@@ -747,19 +753,24 @@
             c.wait()
 
 
-def last(tokens, cotangent, selected, new_block, new_grad, sums, hidden):
+def last(tokens, cotangent, selected, new_block, new_grad, small, sums, hidden):
     rows, spots, width = tokens.shape
     chosen = selected.shape[1]
     cut = 1024
     big = pl.BlockSpec(memory_space=pl.ANY)
     table = pl.BlockSpec((1, cut, width), lambda r, i: (r, i, 0))
     fresh = pl.BlockSpec((chosen, width), lambda r, i: (r, 0))
+    vectors = (width, width, width, width, hidden)
+
+    def whole(shape):
+        return pl.BlockSpec(shape, lambda r, i: (0,) * len(shape))
+
     n_copies = hidden // PIECE * (width // 128) + hidden // 128 + 4 * (width // 128)
     return pl.pallas_call(
         last_kernel,
         grid=(rows, spots // cut),
-        in_specs=[pl.BlockSpec(selected.shape, lambda r, i: (0, 0)), table, table, fresh, fresh, big],
-        out_specs=[table, table, big, big, big, big],
+        in_specs=[whole(selected.shape), table, table, fresh, fresh, whole(small.shape), big],
+        out_specs=[table, table, big, big, big, big] + [whole((n,)) for n in vectors],
         out_shape=[
             jax.ShapeDtypeStruct(tokens.shape, BF16),
             jax.ShapeDtypeStruct(tokens.shape, BF16),
@@ -767,6 +778,7 @@
             jax.ShapeDtypeStruct((width, width), F32),
             jax.ShapeDtypeStruct((width, hidden), F32),
             jax.ShapeDtypeStruct((hidden, width), F32),
+            *(jax.ShapeDtypeStruct((n,), F32) for n in vectors),
         ],
         scratch_shapes=[
             pltpu.VMEM(sums.shape, F32),
@@ -774,7 +786,7 @@
             pltpu.SemaphoreType.DMA((n_copies,)),
         ],
         compiler_params=pltpu.CompilerParams(vmem_limit_bytes=63 * 2**20),
-    )(selected, tokens, cotangent, new_block, new_grad, sums)
+    )(selected, tokens, cotangent, new_block, new_grad, small, sums)
 
 
 def body(
@@ -785,11 +797,10 @@
     sums, small, new_block, new_grad = device_sums(
         mesh, made, (w_qkv, w_out, w_up, w_down), (b_up, b_down, w_router, gain_attn, gain_mlp)
     )
-    block_out, grad_tokens, grad_qkv, grad_out, grad_up, grad_down = last(
-        tokens, cotangent, selected, new_block, new_grad, sums.reshape(-1, 128), hidden
+    block_out, grad_tokens, grad_qkv, grad_out, grad_up, grad_down, *vectors = last(
+        tokens, cotangent, selected, new_block, new_grad, small, sums.reshape(-1, 128), hidden
     )
-    grad_b_up = small[32:].reshape(-1, 8, 128)[:, : PIECE // 128].reshape(-1)
-    grad_router, grad_gain_attn, grad_gain_mlp, grad_b_down = (small[i : i + 6].reshape(-1) for i in (0, 8, 16, 24))
+    grad_router, grad_gain_attn, grad_gain_mlp, grad_b_down, grad_b_up = vectors
     return (
         block_out,
         grad_tokens,

time: 296 us -> 293 us (0.990)
  no operation moved by 1% of the time
where the time goes in v3:
time: 293 us
  Pallas kernels  292 us (100%)
    pallas_call x1, Pallas kernels, device_sums(): pl.pallas_call(functools.partial(sums_kernel, dict(dims=dims, lags=lags,...  227 us
    pallas_call x1, Pallas kernels, last(): pl.pallas_call(last_kernel, grid=(rows, spots // cut), in_specs=[whole(se...  37.2 us
    pallas_call x1, Pallas kernels, first(): pl.pallas_call(first_kernel, grid=(rows,), in_specs=[pl.BlockSpec(memory_...  28.3 us

profile of v3, /device:TPU:0, one launch (start us, length us, event | category | flops | bytes accessed | tf_op | source)
XLA Modules:
  0.0 293.1 jit_solution(11751077107520150033)
XLA Ops:
  0.6 28.3 %shard_map.212 = (bf16[1024,768]{1,0:T(8,128)(2,1)}, bf16[1024,768]{1,0:T(8,128)(2,1)}, bf16[1024,768]{1,0:T(8,128)(2,1)}, bf16[1024,768]{1,0:T(8,128)(2,1)}, bf...) custom-call(s32[4,16]{1,0:T(4,128)} %lens.1, ...), custom_call_target="tpu_custom_call" | custom-call | tf_op jit(solution)/shard_map/pallas_call | solution.py:150
  28.9 226.8 %shard_map.213 = (f32[27,2,1024,128]{3,2,1,0:T(8,128)}, f32[80,128]{1,0:T(8,128)}, bf16[1024,768]{1,0:T(8,128)(2,1)}, bf16[1024,768]{1,0:T(8,128)(2,1)}) custom-call(bf16[1024,768]{1,0:T(8,128)(2,1)} %get-tuple-element.37.nm_h, bf16[1024,768]{1,0:T(8,128)(2,1)} %get-tuple-element.38.dmix_h, bf16[1024,768]{1,0:T(8,128)(2,1)} %get-tuple-element.39.normed_h, ...), custom_call_target="tpu_custom_call" | custom-call | tf_op jit(solution)/shard_map/pallas_call | solution.py:635
  255.7 37.2 %shard_map.214 = (bf16[4,2048,768]{2,1,0:T(8,128)(2,1)}, bf16[4,2048,768]{2,1,0:T(8,128)(2,1)}, f32[768,2304]{1,0:T(8,128)}, f32[768,768]{1,0:T(8,128)}, f32[768...) custom-call(s32[4,256]{1,0:T(4,128)} %selected.3, ...), custom_call_target="tpu_custom_call" | custom-call | tf_op jit(solution)/shard_map/pallas_call | solution.py:769
